TPU v7x, 128 devices: a whole 4x4x4 slice. The times are simulated.
128 devices in a mesh: row: 8 (over z, x_lo), col: 16 (over x_hi, y, core).
Axes of the slice: x: 4 (x_hi: 2, x_lo: 2; x = x_hi * 2 + x_lo), y: 4, z: 4, core: 2. Of those that a mesh axis runs over, the one named last changes fastest.
Arguments:
- integrals: bfloat16 [12800, 6400], P(None, 'col'), may hold values from -0.109375 to 0.109375
- packed_store: bfloat16 [9216, 50, 50], P(('row', 'col')), may hold values from -6 to 6
- pair_sector: int32 [6400], replicated, may hold values from 0 to 1
- owner_map: int32 [128], replicated, may hold values from 0 to 127, each once
Outputs:
- cycle_term: bfloat16 [12800, 6400], P('col', 'row')
Inputs may be any that keep to these rules, and one draw needn't show every extreme that they name: owner_map is a permutation of the devices.
All inputs are finite; a program needn't handle non-finite values.
Results may differ from a plain program's by a relative error of at most 0.001.
Values may be sent and summed in bfloat16 or wider, within the bound.
A program may use at most 192 MiB of HBM per device.

v0:
```python
import jax
import jax.numpy as jnp
from jax import lax
from jax.sharding import PartitionSpec as P


def ceil_div(numer, denom):
    return -(-numer // denom)


def block_positions(owner_map, brow, bcol, row_devices, col_devices, slot_count):
    device_total = row_devices * col_devices
    lower_end = jnp.minimum(brow, bcol)
    upper_end = jnp.maximum(brow, bcol)
    class_row = lower_end % row_devices
    class_col = upper_end % col_devices
    tile_down = lower_end // row_devices
    tile_across = upper_end // col_devices
    earlier_tiles = jnp.arange(col_devices, dtype=jnp.int32)
    need = class_row[..., None] + row_devices * earlier_tiles - class_col[..., None]
    first_ok = jnp.clip(ceil_div(need, col_devices), 0, row_devices)
    per_tile = row_devices - first_ok
    before = jnp.sum(jnp.where(earlier_tiles < tile_down[..., None], per_tile, 0), axis=-1)
    first_same = jnp.clip(
        ceil_div(class_row + row_devices * tile_down - class_col, col_devices), 0, row_devices
    )
    within = jnp.maximum(tile_across - first_same, 0)
    slot_index = before + within
    class_index = class_row * col_devices + class_col
    devices_all = jnp.arange(device_total, dtype=jnp.int32)
    owner_index = jnp.sum(jnp.where(class_index[..., None] == devices_all, owner_map, 0), axis=-1)
    return owner_index * slot_count + slot_index


def body(integrals, packed_store, pair_sector, owner_map):
    row_devices = lax.axis_size("row")
    col_devices = lax.axis_size("col")
    device_total = row_devices * col_devices
    slot_count = packed_store.shape[0]
    block_side = packed_store.shape[1]
    block_area = block_side * block_side
    capacity = 1 + col_devices // row_devices
    my_row = lax.axis_index("row")
    my_col = lax.axis_index("col")
    myself = my_row * col_devices + my_col
    target_dev = jnp.arange(device_total, dtype=jnp.int32)[:, None]
    local_pos = jnp.arange(device_total, dtype=jnp.int32)[None, :]
    send_brow = row_devices * (target_dev % col_devices) + local_pos // col_devices
    send_bcol = col_devices * (target_dev // col_devices) + local_pos % col_devices
    source_pos = block_positions(
        owner_map, send_brow, send_bcol, row_devices, col_devices, slot_count
    )
    is_mine = (source_pos // slot_count == myself).astype(jnp.int32)
    positions_all = jnp.arange(device_total, dtype=jnp.int32)
    before_mask = (positions_all[:, None] < positions_all[None, :]).astype(jnp.int32)
    send_rank = jnp.sum(is_mine[:, :, None] * before_mask[None, :, :], axis=1)
    cap_slots = jnp.arange(capacity, dtype=jnp.int32)
    selector = is_mine[:, None, :] * (send_rank[:, None, :] == cap_slots[None, :, None]).astype(
        jnp.int32
    )
    slot_pick = jnp.sum(selector * (source_pos % slot_count)[:, None, :], axis=2)
    flip_pick = jnp.sum(selector * (send_brow > send_bcol).astype(jnp.int32)[:, None, :], axis=2)
    diag_pick = jnp.sum(selector * (send_brow == send_bcol).astype(jnp.int32)[:, None, :], axis=2)
    is_valid = jnp.sum(selector, axis=2)
    slot_range = jnp.arange(slot_count, dtype=jnp.int32)
    pick_table = (
        (slot_pick[:, :, None] == slot_range[None, None, :]) & (is_valid[:, :, None] > 0)
    ).astype(jnp.bfloat16)
    picked = jnp.dot(
        pick_table.reshape(device_total * capacity, slot_count),
        packed_store.reshape(slot_count, block_area),
        preferred_element_type=jnp.float32,
    )
    chosen = picked.astype(jnp.bfloat16).reshape(device_total, capacity, block_side, block_side)
    flipped = jnp.swapaxes(chosen, 2, 3)
    inner_rows = jnp.arange(block_side, dtype=jnp.int32)[None, None, :, None]
    inner_cols = jnp.arange(block_side, dtype=jnp.int32)[None, None, None, :]
    mirrored = jnp.where(inner_rows <= inner_cols, chosen, flipped)
    outgoing = jnp.where(
        (flip_pick > 0)[:, :, None, None],
        flipped,
        jnp.where((diag_pick > 0)[:, :, None, None], mirrored, chosen),
    )
    used_width = capacity * block_area
    padded_width = (used_width + 127) // 128 * 128
    flat_send = jnp.pad(
        outgoing.reshape(device_total, used_width), ((0, 0), (0, padded_width - used_width))
    )
    received = lax.all_to_all(flat_send, ("row", "col"), split_axis=0, concat_axis=0, tiled=True)
    incoming = received[:, :used_width].reshape(device_total * capacity, block_area)
    tile_pos = jnp.arange(device_total, dtype=jnp.int32)
    own_brow = row_devices * my_col + tile_pos // col_devices
    own_bcol = col_devices * my_row + tile_pos % col_devices
    own_source = (
        block_positions(owner_map, own_brow, own_bcol, row_devices, col_devices, slot_count)
        // slot_count
    )
    earlier = (tile_pos[:, None] > tile_pos[None, :]) & (own_source[:, None] == own_source[None, :])
    own_rank = jnp.sum(earlier.astype(jnp.int32), axis=1)
    incoming_index = own_source * capacity + own_rank
    incoming_range = jnp.arange(device_total * capacity, dtype=jnp.int32)
    take_table = (incoming_index[:, None] == incoming_range[None, :]).astype(jnp.bfloat16)
    tile_blocks = jnp.dot(take_table, incoming, preferred_element_type=jnp.float32).astype(
        jnp.bfloat16
    )
    local_amp = tile_blocks.reshape(row_devices, col_devices, block_side, block_side)
    local_amp = local_amp.transpose(0, 2, 1, 3).reshape(
        row_devices * block_side, col_devices * block_side
    )
    row_sector = lax.dynamic_slice_in_dim(
        pair_sector, my_col * row_devices * block_side, row_devices * block_side, 0
    )
    col_sector = lax.dynamic_slice_in_dim(
        pair_sector, my_row * col_devices * block_side, col_devices * block_side, 0
    )
    local_amp = jnp.where(
        row_sector[:, None] == col_sector[None, :], local_amp, jnp.zeros((), jnp.bfloat16)
    )
    result = lax.psum_scatter(
        jnp.dot(integrals, local_amp, preferred_element_type=jnp.float32),
        "col",
        scatter_dimension=0,
        tiled=True,
    )
    return result.astype(jnp.bfloat16)


def solution(mesh):
    in_specs = (P(None, "col"), P(("row", "col"), None, None), P(), P())
    out_specs = P("col", "row")
    return jax.shard_map(body, mesh=mesh, in_specs=in_specs, out_specs=out_specs, check_vma=False)
```

profile of v0, /device:TPU:1, one launch (start us, length us, event | category | flops | bytes accessed | tf_op | source)
XLA Modules:
  0.0 509.9 jit_solution(8700768865189984081)
XLA Ops:
  6.9 5.8 %select_reduce_fusion = s32[128,128]{1,0:T(8,128)S(1)} fusion(s32[128]{0:T(128)} %param.7, s32[128,128]{1,0:T(8,128)S(1)} %get-tuple-element.13), kind=kLoop, calls=%fused_computation.2 | loop fusion | flops 6275072 | bytes 131584 | tf_op jit(solution)/shard_map/reduce_sum | solution.py:31
  12.7 1.2 fusion.7
  13.8 0.3 add_select_fusion.1
  14.2 3.1 multiply_reduce_fusion
  18.6 1.4 reshape.1036
  20.0 1.0 convolution_convert_fusion
  20.9 2.5 copy.31
  23.4 8.5 %reshape.1037 = bf16[128,3,50,50]{3,2,1,0:T(8,128)(2,1)} reshape(bf16[384,2500]{1,0:T(8,128)(2,1)} %copy.31) | data formatting | bytes 3840000 | tf_op jit(solution)/shard_map/reshape | solution.py:74
  31.9 8.5 %copy.32 = bf16[128,3,50,50]{2,3,1,0:T(8,128)(2,1)} copy(bf16[128,3,50,50]{3,2,1,0:T(8,128)(2,1)} %reshape.1037) | data formatting | bytes 3840000 | tf_op jit(solution)/shard_map/reshape | solution.py:74
  40.4 7.9 %fusion = bf16[128,3,50,50]{3,2,1,0:T(8,128)(2,1)} fusion(bf16[128,3,50,50]{3,2,1,0:T(8,128)(2,1)} %reshape.1037, bf16[128,3,50,50]{2,3,1,0:T(8,128)(2,1)} %copy.32, pred[50,50]{1,0:T(8,128)(4,1)S(1)} %iota_compare_fusion.9, pred[128,3]{1,0:T(8,128)(4,1)S(1)} %copy.33, pred[128,3]{1,0:T(8,128)(4,1)S(1)} %copy.28), kind=kLoop, calls=%fused_computation.5 | loop fusion | flops 2880000 | bytes 5763268 | tf_op jit(solution)/shard_map/jit(_where)/select_n | solution.py:79
  48.3 6.2 %reshape.1042 = bf16[128,7500]{1,0:T(8,128)(2,1)S(1)} reshape(bf16[128,3,50,50]{3,2,1,0:T(8,128)(2,1)} %fusion) | data formatting | bytes 3840000 | tf_op jit(solution)/shard_map/reshape | solution.py:87
  54.5 2.3 copy.39
  56.8 1.7 pad_bitcast_fusion
  58.5 0.5 broadcast.1822
  59.0 2.8 reduce
  61.8 2.8 copy.45
  64.6 3.0 reshape.1045
  67.6 11.5 %all-to-all-start = ((bf16[128,2,3776]{2,1,0:T(2,128)(2,1)}), bf16[128,2,3776]{2,1,0:T(2,128)(2,1)S(1)}, u32[]{:S(2)}, u32[]{:S(2)}) async-start(bf16[128,2,3776]{2,1,0:T(2,128)(2,1)} %reshape.1045), calls=%async_computation | async-start | bytes 3932160 | tf_op jit(solution)/shard_map/all_to_all | solution.py:89
  79.3 0.8 dynamic_slice.6
  80.1 0.8 dynamic_slice.7
  81.4 26.2 %all-to-all-done = bf16[128,2,3776]{2,1,0:T(2,128)(2,1)S(1)} async-done(((bf16[128,2,3776]{2,1,0:T(2,128)(2,1)}), bf16[128,2,3776]{2,1,0:T(2,128)(2,1)S(1)}, u32[]{:S(2)}, u32[]{:S(2)}) %all-to-all-start) | async-done | bytes 1933344 | tf_op jit(solution)/shard_map/all_to_all | solution.py:89
  107.6 7.3 %reshape.1046 = bf16[128,1,7552]{2,1,0:T(2,128)(2,1)} reshape(bf16[128,2,3776]{2,1,0:T(2,128)(2,1)S(1)} %all-to-all-done) | data formatting | bytes 3866624
  115.0 3.6 copy.44
  118.6 3.8 reshape.1039
  122.3 1.0 convolution_convert_fusion.1
  123.6 1.7 reshape.1040
  125.6 1.8 reshape.1041
  127.3 21.2 %convolution_bitcast_fusion = f32[12800,800]{0,1:T(8,128)} fusion(bf16[12800,400]{0,1:T(8,128)(2,1)} %param.4, bf16[400,800]{1,0:T(8,128)(2,1)S(1)} %reshape.1041, s32[800]{0:T(1024)S(1)} %dynamic_slice.7, s32[400]{0:T(512)S(1)} %dynamic_slice.6), kind=kOutput, calls=%fused_computation | convolution fusion | flops 8192640000 | bytes 51844800 | tf_op jit(solution)/shard_map/dot_general | solution.py:120
  148.5 45.5 %copy.40 = f32[12800,800]{1,0:T(8,128)} copy(f32[12800,800]{0,1:T(8,128)} %convolution_bitcast_fusion) | data formatting | bytes 81920000
  194.1 303.7 %reduce-scatter.4.cloned.1.call-done = f32[800,800]{1,0:T(8,128)} async-done(((f32[12800,800]{1,0:T(8,128)}), f32[800,800]{1,0:T(8,128)}) %reduce-scatter.4.cloned.1.call-update) | async-done | bytes 2560016
  497.7 3.0 copy.41
  500.8 2.2 copy.38
  (31 shorter events, 2.9 us)
Async XLA Ops:
  67.6 13.4 %copy-start = (s32[128]{0:T(128)S(1)}, s32[128]{0:T(128)}, u32[]{:S(2)}) copy-start(s32[128]{0:T(128)} %param.7) | copy-start | bytes 1540
  67.6 40.0 %all-to-all-start = ((bf16[128,2,3776]{2,1,0:T(2,128)(2,1)}), bf16[128,2,3776]{2,1,0:T(2,128)(2,1)S(1)}, u32[]{:S(2)}, u32[]{:S(2)}) async-start(bf16[128,2,3776]{2,1,0:T(2,128)(2,1)} %reshape.1045), calls=%async_computation | async-start | bytes 3932160 | tf_op jit(solution)/shard_map/all_to_all | solution.py:89
  79.1 418.6 %reduce-scatter.4.cloned.1.call-start = ((), (), s32[]{:S(2)}) async-start(), calls=%async_computation.2 | async-start | bytes 48742400
Sparse Core Ops, SparseCore 0:
  194.2 303.5 reduce-scatter.3
where the time goes:
time: 512 us; the launch traced here: 510 us
  waiting for transfers between devices  330 us (64%)
  local copies, waits for them, and re-layouts  109 us (21%)
  matrix products  23.2 us (5%)
  other arithmetic  22.2 us (4%)
  between operations  13.6 us (3%)
  starting transfers between devices  11.7 us (2%)
    unnamed x2, waiting for transfers between devices  304 us
    unnamed x8, local copies, waits for them, and re-layouts  65.3 us
    all_to_all x1, waiting for transfers between devices, body(): lax.all_to_all(flat_send, ('row', 'col'), split_axis=0, concat_axis=0, ti...  26.2 us
    dot_general x1, matrix products, body(): jnp.dot(integrals, local_amp, preferred_element_type=jnp.float32)  21.2 us
    reshape x2, local copies, waits for them, and re-layouts, body(): picked.astype(jnp.bfloat16)  17 us
    all_to_all x1, starting transfers between devices, body(): lax.all_to_all(flat_send, ('row', 'col'), split_axis=0, concat_axis=0, ti...  11.5 us
  transfers between devices with their start and end apart: 2, of which 2 were waited for; matrix products, arithmetic and copies ran while one was open for 0% of the time, Pallas kernels for 0%

commit v1 on v0

v1 whole, which is shorter than its diff:
```python
import jax
import jax.numpy as jnp
from jax import lax
from jax.experimental import pallas as pl
from jax.experimental.pallas import tpu as pltpu
from jax.sharding import PartitionSpec as P

MESH = pl.DeviceIdType.MESH
BF = jnp.bfloat16
F32 = jnp.float32

TILE = 800
KB = 400
MAIN = 384
REM = 16
PIECE = 208
SLOT = PIECE + REM
ROWS = 4 * SLOT
NPAD = 896
OFFS = [(0, 1), (0, 3), (1, 1), (1, 3), (0, 2), (1, 2)]


def piece_start(q):
    return 192 * q + 16 * (q // 3)


def kernel(slots, owner, integrals, packed, mask, out,
           sendbuf, mid, fin, rem_in, stage, stage_full, irecv, arecv,
           x_buf, e1, e2, s_buf, st_buf, acc, l_buf, arem,
           lsem, rsem, s1_send, s1_recv, s2_send, s2_recv, p1_send, p1_recv, full_send, full_recv,
           z_send, z_recv, z2_send, z2_recv, ex_send, ex_recv, a_send, a_recv):
    r = lax.axis_index("row")
    c = lax.axis_index("col")
    z, xl = r // 2, r % 2
    xh, y, k = c // 8, (c // 2) % 4, c % 2

    def col(xh_, y_, k_):
        return xh_ * 8 + (y_ % 4) * 2 + k_

    def remote(src, dst, ssem, rsem_, row_, col_):
        return pltpu.make_async_remote_copy(src_ref=src, dst_ref=dst, send_sem=ssem, recv_sem=rsem_,
                                            device_id=(row_, col_), device_id_type=MESH)

    sends = []

    def send(cp):
        cp.start()
        sends.append(cp)

    mate = c + 1 - 2 * k
    cross_c = c + 8 - 16 * xh
    row_flip = z * 2 + 1 - xl

    local = []

    def fetch(i, cc, q, dst):
        start = pl.multiple_of(cc * TILE + piece_start(q), 16)
        a = pltpu.make_async_copy(integrals.at[pl.ds(start, PIECE), pl.ds(0, MAIN)], dst, lsem.at[i])
        b = pltpu.make_async_copy(integrals.at[pl.ds(start, PIECE), pl.ds(MAIN, REM)], rem_in.at[i], rsem.at[i])
        a.start()
        b.start()
        local.append((a, b))

    n = 0
    for o, (dxh, dy) in enumerate(OFFS):
        for kk in range(2):
            cc = col(xh + dxh - 2 * xh * dxh, y + dy, kk)
            fetch(n, cc, z, stage.at[n, pl.ds(0, PIECE), :])
            n += 1
    full_c = [mate, col(1 - xh, y, 0), col(1 - xh, y, 1)]
    for f in range(3):
        for q in range(4):
            fetch(n, full_c[f], q, stage_full.at[f, pl.ds(q * SLOT, PIECE), :])
            n += 1
    for q in range(4):
        fetch(n, c, q, irecv.at[c, pl.ds(q * SLOT, PIECE), :])
        n += 1

    for cc in range(16):
        def pick(rr, carry):
            sendbuf[cc, rr] = packed[slots[rr * 16 + cc]]
            return carry
        lax.fori_loop(0, 8, pick, 0, unroll=True)
    for d in range(1, 16):
        cc = (c + d) % 16
        send(remote(sendbuf.at[cc], mid.at[:, c], s1_send.at[d], s1_recv.at[d], r, cc))
    own1 = pltpu.make_async_copy(sendbuf.at[c], mid.at[:, c], s1_send.at[0])
    own1.start()

    eye = (lax.broadcasted_iota(jnp.int32, (REM, REM), 0) == lax.broadcasted_iota(jnp.int32, (REM, REM), 1)).astype(BF)

    def add_rem(i, ref, row0):
        a, b = local[i]
        a.wait()
        b.wait()
        t = lax.dot_general(eye, rem_in[i], (((1,), (1,)), ((), ())), preferred_element_type=F32)
        ref[pl.ds(row0, REM), :] = jnp.zeros((REM, MAIN), BF)
        ref[pl.ds(row0, REM), pl.ds(0, PIECE)] = t.astype(BF)

    n = 0
    zrow = pl.multiple_of(z * SLOT, 16)
    for o, (dxh, dy) in enumerate(OFFS):
        for kk in range(2):
            add_rem(n, stage.at[n], PIECE)
            cc = col(xh + dxh - 2 * xh * dxh, y + dy, kk)
            rr = row_flip if dxh else r
            send(remote(stage.at[n], irecv.at[c, pl.ds(zrow, SLOT), :], p1_send.at[n], p1_recv.at[o, k], rr, cc))
            n += 1
    for f in range(3):
        for q in range(4):
            add_rem(n, stage_full.at[f], q * SLOT + PIECE)
            n += 1
        send(remote(stage_full.at[f], irecv.at[c], full_send.at[f],
                    full_recv.at[0] if f == 0 else full_recv.at[1 + k], r if f == 0 else row_flip, full_c[f]))
    for q in range(4):
        add_rem(n, irecv.at[c], q * SLOT + PIECE)
        n += 1

    def table(b, carry):
        j = lax.broadcasted_iota(jnp.int32, (128, NPAD), 0)
        col_i = lax.broadcasted_iota(jnp.int32, (128, NPAD), 1) - 50 * b
        e1[pl.ds(pl.multiple_of(b * 128, 128), 128), :] = jnp.where((j < 50) & (col_i == j), 1.0, 0.0).astype(BF)
        e2[pl.ds(pl.multiple_of(b * 128, 128), 128), :] = jnp.where(
            (j >= 50) & (j < 100) & (col_i == j - 50), 1.0, 0.0).astype(BF)
        return carry
    lax.fori_loop(0, 16, table, 0)
    s_buf[pl.ds(TILE, NPAD - TILE), :] = jnp.zeros((NPAD - TILE, NPAD), BF)

    def src_col(o, kk):
        dxh, dy = OFFS[o]
        return col(xh + dxh - 2 * xh * dxh, y + 4 - dy, kk)

    up, down = ((z + 1) % 4) * 2 + xl, ((z + 3) % 4) * 2 + xl
    zrows = [pl.multiple_of(((z + d) % 4) * SLOT, 16) for d in range(4)]

    def i_slot(o, kk, d):
        return irecv.at[src_col(o, kk), pl.ds(zrows[d], SLOT), :]

    def share(o):
        for kk in range(2):
            ref = i_slot(o, kk, 0)
            remote(ref, ref, p1_send.at[0], p1_recv.at[o, kk], r, c).wait_recv()
            send(remote(ref, ref, z_send.at[o, kk, 0], z_recv.at[o, kk, 0], up, c))
            send(remote(ref, ref, z_send.at[o, kk, 1], z_recv.at[o, kk, 1], down, c))

    def pass_on(o):
        for kk in range(2):
            lo, hi = i_slot(o, kk, 3), i_slot(o, kk, 1)
            first, second = ((lo, 0), (hi, 1)) if kk == 0 else ((hi, 1), (lo, 0))
            remote(first[0], first[0], z_send.at[o, kk, 0], z_recv.at[o, kk, first[1]], r, c).wait_recv()
            send(remote(first[0], first[0], z2_send.at[o, kk], z2_recv.at[o, kk], up if kk == 0 else down, c))
        for kk in range(2):
            lo, hi = i_slot(o, kk, 3), i_slot(o, kk, 1)
            second = (hi, 1) if kk == 0 else (lo, 0)
            remote(second[0], second[0], z_send.at[o, kk, 0], z_recv.at[o, kk, second[1]], r, c).wait_recv()

    def arrived(o):
        for kk in range(2):
            ref = i_slot(o, kk, 2)
            remote(ref, ref, z_send.at[o, kk, 0], z2_recv.at[o, kk], r, c).wait_recv()

    own1.wait()
    for d in range(1, 16):
        cc = (c + 16 - d) % 16
        remote(sendbuf.at[0], mid.at[:, cc], s1_send.at[d], s1_recv.at[d], r, c).wait_recv()
    for d in range(1, 8):
        rr = (r + d) % 8
        send(remote(mid.at[rr], fin.at[pl.ds(pl.multiple_of(r * 16, 16), 16)], s2_send.at[d], s2_recv.at[d], rr, c))
    own2 = pltpu.make_async_copy(mid.at[r], fin.at[pl.ds(pl.multiple_of(r * 16, 16), 16)], s2_send.at[0])
    own2.start()

    share(0)
    share(1)

    own2.wait()
    for d in range(1, 8):
        rr = (r + 8 - d) % 8
        remote(mid.at[0], fin.at[pl.ds(pl.multiple_of(rr * 16, 16), 16)], s2_send.at[d], s2_recv.at[d], r, c).wait_recv()

    def put(a, carry):
        for b in range(16):
            x_buf[pl.ds(pl.multiple_of(32 * a, 32), 32), pl.ds(128 * b, 128)] = fin[owner[16 * a + b]]
        return carry
    lax.fori_loop(0, 8, put, 0)
    m_i = lax.broadcasted_iota(jnp.int32, (KB, 256), 0)
    n_i = lax.broadcasted_iota(jnp.int32, (KB, 256), 1)
    blk = (m_i * 1311) >> 16
    inner = m_i - 50 * blk
    f1 = jnp.where((inner < 32) & (n_i == 32 * blk + inner), 1.0, 0.0).astype(BF)
    f2 = jnp.where((inner >= 32) & (n_i == 32 * blk + inner - 32), 1.0, 0.0).astype(BF)
    own_half = s_buf.at[pl.ds(pl.multiple_of(k * KB, 16), KB), :]
    mate_half = s_buf.at[pl.ds(pl.multiple_of((1 - k) * KB, 16), KB), :]
    def place(i, carry):
        at = pl.ds(pl.multiple_of(i * 128, 128), 128)
        y1 = jnp.dot(x_buf[...], e1[:, at], preferred_element_type=F32).astype(BF)
        y2 = jnp.dot(x_buf[...], e2[:, at], preferred_element_type=F32).astype(BF)
        part = jnp.dot(f1, y1, preferred_element_type=F32) + jnp.dot(f2, y2, preferred_element_type=F32)
        s_buf[pl.ds(pl.multiple_of(k * KB, 16), KB), at] = part.astype(BF)
        return carry
    lax.fori_loop(0, 7, place, 0)
    send(remote(own_half, own_half, ex_send.at[0], ex_recv.at[0], r, mate))
    share(2)
    remote(mate_half, mate_half, ex_send.at[0], ex_recv.at[0], r, c).wait_recv()
    def turn(i, carry):
        at = pl.ds(pl.multiple_of(i * 128, 128), 128)
        st_buf[:, at] = s_buf[at, pl.ds(pl.multiple_of(k * MAIN, 128), 512)].T
        return carry
    lax.fori_loop(0, 7, turn, 0)

    def choose(i, carry):
        row0 = pl.multiple_of(i * 80, 16)
        straight = s_buf[pl.ds(pl.multiple_of(k * KB + row0, 16), 80), :]
        flipped = st_buf[pl.ds(pl.multiple_of(16 * k + row0, 16), 80), :]
        g_k = lax.broadcasted_iota(jnp.int32, (80, NPAD), 0) + (c * KB + row0)
        g_n = lax.broadcasted_iota(jnp.int32, (80, NPAD), 1) + r * TILE
        tile = jnp.where(g_k <= g_n, straight.astype(F32), flipped.astype(F32))
        tile = jnp.where(mask[pl.ds(row0, 80), :] > 0, tile, 0.0)
        arecv[c, pl.ds(row0, 80), :] = tile.astype(BF)
        return carry
    lax.fori_loop(0, 5, choose, 0)

    yup, ydown = col(xh, y + 1, k), col(xh, y + 3, k)

    def a_send_to(cc, i, j, dest):
        send(remote(arecv.at[cc], arecv.at[cc], a_send.at[i], a_recv.at[j], r, dest))

    def a_wait(cc, j):
        remote(arecv.at[cc], arecv.at[cc], a_send.at[0], a_recv.at[j], r, c).wait_recv()

    def xy(dxh, dy, kk):
        return col(xh + dxh - 2 * xh * dxh, y + dy + 4, kk)

    a_send_to(c, 0, 1, yup)
    a_send_to(c, 1, 2, ydown)
    a_send_to(c, 2, 0, cross_c)
    a_send_to(c, 3, 8, mate)

    def product(cc, first=False):
        def cut(n0, nw):
            part = jnp.dot(irecv[cc], arecv[cc, pl.ds(0, MAIN), pl.ds(n0, nw)], preferred_element_type=F32)
            if first:
                acc[:, pl.ds(n0, nw)] = part
            else:
                acc[:, pl.ds(n0, nw)] += part

        def step(i, carry):
            cut(pl.multiple_of(i * 256, 256), 256)
            return carry
        lax.fori_loop(0, 3, step, 0)
        cut(768, 128)

    product(c, True)
    share(3)
    share(4)
    share(5)
    a_wait(cross_c, 0)
    a_send_to(cross_c, 4, 3, yup)
    a_send_to(cross_c, 5, 4, ydown)
    a_send_to(cross_c, 6, 9, mate)
    pass_on(0)
    pass_on(1)
    a_wait(xy(0, -1, k), 1)
    a_send_to(xy(0, -1, k), 7, 5, yup)
    a_send_to(xy(0, -1, k), 8, 10, mate)
    a_wait(xy(0, 1, k), 2)
    a_send_to(xy(0, 1, k), 9, 11, mate)
    full = irecv.at[mate]
    remote(full, full, full_send.at[0], full_recv.at[0], r, c).wait_recv()
    a_wait(mate, 8)
    product(mate)
    for kk in range(2):
        full = irecv.at[xy(1, 0, kk)]
        remote(full, full, full_send.at[0], full_recv.at[1 + kk], r, c).wait_recv()
    product(cross_c)
    a_wait(xy(1, 0, 1 - k), 9)
    product(xy(1, 0, 1 - k))
    pass_on(2)
    pass_on(3)
    a_wait(xy(1, 1, k), 4)
    a_send_to(xy(1, 1, k), 10, 6, ydown)
    a_send_to(xy(1, 1, k), 11, 12, mate)
    a_wait(xy(1, -1, k), 3)
    a_send_to(xy(1, -1, k), 12, 13, mate)
    pass_on(4)
    pass_on(5)
    arrived(0)
    arrived(1)
    for dy, j in ((-1, 10), (1, 11)):
        product(xy(0, dy, k))
        a_wait(xy(0, dy, 1 - k), j)
        product(xy(0, dy, 1 - k))
    a_wait(xy(0, 2, k), 5)
    a_send_to(xy(0, 2, k), 13, 14, mate)
    arrived(2)
    arrived(3)
    for dy, j in ((1, 12), (-1, 13)):
        product(xy(1, dy, k))
        a_wait(xy(1, dy, 1 - k), j)
        product(xy(1, dy, 1 - k))
    a_wait(xy(1, 2, k), 6)
    a_send_to(xy(1, 2, k), 14, 15, mate)
    arrived(4)
    arrived(5)
    product(xy(0, 2, k))
    product(xy(1, 2, k))
    a_wait(xy(0, 2, 1 - k), 14)
    product(xy(0, 2, 1 - k))
    a_wait(xy(1, 2, 1 - k), 15)
    product(xy(1, 2, 1 - k))

    for cc in range(16):
        arem[pl.ds(16 * cc, 16), :] = arecv[cc, pl.ds(MAIN, REM), :]
        for q in range(4):
            l_buf[q, pl.ds(16 * cc, 16), :] = irecv[cc, pl.ds(q * SLOT + PIECE, REM), pl.ds(0, 256)]
    for q, (skip, row0) in enumerate(((0, 0), (16, 208), (16, 400), (0, 592))):
        part = lax.dot_general(l_buf[q], arem[...], (((0,), (0,)), ((), ())), preferred_element_type=F32)
        rows = PIECE - skip
        total = acc[pl.ds(q * SLOT + skip, rows), pl.ds(0, TILE)] + part[skip:PIECE, :TILE]
        out[pl.ds(row0, rows), :] = total.astype(BF)

    for cp in sends:
        cp.wait_send()


def slot_table(owner_map, me):
    index = jnp.arange(128, dtype=jnp.int32)
    mine = jnp.sum(jnp.where(owner_map == me, index, 0))
    a, b = mine // 16, mine % 16
    rr, cc = index // 16, index % 16
    lo, hi, h = jnp.minimum(rr, cc // 2), jnp.maximum(rr, cc // 2), cc % 2
    e0 = (a > b).astype(jnp.int32)
    e1 = (a + 8 > b).astype(jnp.int32)
    down = 2 * lo + h
    before = 8 * down - (lo * (lo - 1) + lo * (e0 + e1) + h * (lo + e0))
    first = lo + jnp.where(h == 1, e1, e0)
    return jnp.clip(before + hi - first, 0, 71)


def body(integrals, packed_store, pair_sector, owner_map):
    r = lax.axis_index("row")
    c = lax.axis_index("col")
    slots = slot_table(owner_map, r * 16 + c)
    pad = jnp.zeros((72, 14, 50), BF)
    low = jnp.concatenate([packed_store[:, 32:, :], pad], axis=1)
    packed = jnp.concatenate([packed_store[:, :32, :], low, jnp.zeros((72, 32, 28), BF)], axis=2)
    rows = lax.dynamic_slice_in_dim(pair_sector, c * KB, KB, 0)
    cols = lax.dynamic_slice_in_dim(pair_sector, r * TILE, TILE, 0)
    cols = jnp.pad(cols, (0, NPAD - TILE), constant_values=-1)
    mask = (rows[:, None] == cols[None, :]).astype(F32)
    dma = pltpu.SemaphoreType.DMA
    vm = lambda *s: pltpu.VMEM(s, BF)
    return pl.pallas_call(
        kernel,
        out_shape=jax.ShapeDtypeStruct((TILE, TILE), BF),
        in_specs=[pl.BlockSpec(memory_space=pltpu.SMEM)] * 2 + [pl.BlockSpec(memory_space=pl.ANY)]
        + [pl.BlockSpec(memory_space=pltpu.VMEM)] * 2,
        out_specs=pl.BlockSpec(memory_space=pltpu.VMEM),
        scratch_shapes=[
            vm(16, 8, 32, 128), vm(8, 16, 32, 128), vm(128, 32, 128),
            vm(28, PIECE, REM), vm(12, SLOT, MAIN), vm(3, ROWS, MAIN), vm(16, ROWS, MAIN), vm(16, KB, NPAD),
            vm(256, 2048), vm(2048, NPAD), vm(2048, NPAD), vm(NPAD, NPAD), vm(512, NPAD),
            pltpu.VMEM((ROWS, NPAD), F32), vm(4, 256, 256), vm(256, NPAD),
            dma((28,)), dma((28,)), dma((16,)), dma((16,)), dma((8,)), dma((8,)),
            dma((12,)), dma((6, 2)), dma((3,)), dma((3,)),
            dma((6, 2, 2)), dma((6, 2, 2)), dma((6, 2)), dma((6, 2)), dma((1,)), dma((1,)),
            dma((15,)), dma((16,)),
        ],
        compiler_params=pltpu.CompilerParams(has_side_effects=True, vmem_limit_bytes=60 * 2**20),
        cost_estimate=pl.CostEstimate(flops=2 * 800 * 800 * 6400, bytes_accessed=20_000_000, transcendentals=0),
    )(slots, owner_map, integrals, packed, mask)


def solution(mesh):
    in_specs = (P(None, "col"), P(("row", "col"), None, None), P(), P())
    return jax.shard_map(body, mesh=mesh, in_specs=in_specs, out_specs=P("col", "row"), check_vma=False)
```

time: 512 us -> 157 us (0.31)
  waiting for transfers between devices: 330 us -> 0 us
  Pallas kernels: 0 us -> 127 us
  local copies, waits for them, and re-layouts: 109 us -> 22.2 us
  matrix products: 23.2 us -> 0 us
  other arithmetic: 22.2 us -> 4.43 us
  starting transfers between devices: 11.7 us -> 0 us
  between operations: 13.6 us -> 2.66 us
    unnamed x2 -> x0, waiting for transfers between devices: 304 us -> none
    pallas_call x0 -> x1, Pallas kernels: none -> 127 us  [body(): pl.pallas_call(kernel, out_shape=jax.ShapeDtypeStruct((TILE, TILE), BF),...]
    unnamed x8 -> x4, local copies, waits for them, and re-layouts: 65.3 us -> 19.6 us
    reshape x8 -> x0, local copies, waits for them, and re-layouts: 34.1 us -> none  [the longest x2 17 us: body(): picked.astype(jnp.bfloat16)]
    all_to_all x1 -> x0, waiting for transfers between devices: 26.2 us -> none  [body(): lax.all_to_all(flat_send, ('row', 'col'), split_axis=0, concat_axis=0, ti...]
    dot_general x3 -> x0, matrix products: 23.2 us -> none  [the longest x1 21.2 us: body(): jnp.dot(integrals, local_amp, preferred_element_type=jnp.float32)]
    all_to_all x1 -> x0, starting transfers between devices: 11.5 us -> none  [body(): lax.all_to_all(flat_send, ('row', 'col'), split_axis=0, concat_axis=0, ti...]
    reduce_sum x7 -> x1, other arithmetic: 10.8 us -> 1.35 us  [slot_table(): mine = jnp.sum(jnp.where(owner_map == me, index, 0))]
  transfers between devices with their start and end apart: 2 -> 0, of which waited for: 2 -> 0; matrix products, arithmetic and copies ran while one was open for 0% -> 0% of each run, Pallas kernels for 0% -> 0%
where the time goes in v1:
time: 157 us; the launch traced here: 156 us
  Pallas kernels  127 us (81%)
  local copies, waits for them, and re-layouts  22.2 us (14%)
  other arithmetic  4.43 us (3%)
  between operations  2.66 us (2%)
    pallas_call x1, Pallas kernels, body(): pl.pallas_call(kernel, out_shape=jax.ShapeDtypeStruct((TILE, TILE), BF),...  127 us
    unnamed x4, local copies, waits for them, and re-layouts  19.6 us

profile of v1, /device:TPU:1, one launch (start us, length us, event | category | flops | bytes accessed | tf_op | source)
XLA Modules:
  0.0 156.4 jit_solution(12952693561917799761)
XLA Ops:
  0.0 0.0 slice-start
  0.0 1.3 fusion.4
  4.0 0.6 fusion.8.slots
  4.6 0.1 pad.8.clone
  4.7 0.8 dynamic_slice.6
  5.4 0.8 dynamic_slice.7
  6.2 1.0 slice.7
  7.2 0.3 copy.9
  7.5 0.0 slice-done
  7.5 1.0 copy.8
  8.5 1.2 fusion.3.packed
  9.7 1.3 compare_convert_fusion.mask
  10.9 15.7 %copy.7.integrals = bf16[12800,400]{1,0:T(8,128)(2,1)} copy(bf16[12800,400]{0,1:T(8,128)(2,1)} %param.4) | data formatting | bytes 20480000 | tf_op args[0]
  26.7 127.1 %shard_map.46 = bf16[800,800]{1,0:T(8,128)(2,1)} custom-call(s32[128]{0:T(128)} %fusion.8.slots, s32[128]{0:T(128)} %owner.1, bf16[12800,400]{1,0:T(8,128)(2,1)} %copy.7.integrals, bf16[72,32,128]{2,1,0:T(8,128)(2,1)} %fusion.3.packed, f32[400,896]{1,0:T(8,128)} %compare_convert_fusion.mask), custom_call_target="tpu_custom_call" | custom-call | flops 8192000000 | bytes 20000000 | tf_op jit(solution)/shard_map/pallas_call | solution.py:352
  153.8 2.6 %copy.11 = bf16[800,800]{1,0:T(8,128)(2,1)} copy(bf16[800,800]{1,0:T(8,128)(2,1)} %shard_map.46) | data formatting | bytes 2560000
  (2 shorter events, 0.0 us)
Async XLA Ops:
  0.0 7.5 %slice-start = ((bf16[72,50,50]{0,2,1:T(8,128)(2,1)}), bf16[72,32,50]{0,2,1:T(8,128)(2,1)S(1)}, s32[]{:S(2)}) async-start(bf16[72,50,50]{0,2,1:T(8,128)(2,1)} %param.5), calls=%async_computation | async-start | bytes 917504 | tf_op jit(solution)/shard_map/slice | solution.py:345

commit v2 on v1

v2 whole, which is shorter than its diff:
```python
import functools

import jax
import jax.numpy as jnp
from jax import lax
from jax.experimental import pallas as pl
from jax.experimental.pallas import tpu as pltpu
from jax.sharding import PartitionSpec as P

MESH = pl.DeviceIdType.MESH
BF = jnp.bfloat16
F32 = jnp.float32

TILE = 800
KB = 400
MAIN = 384
REM = 16
PIECE = 208
SLOT = PIECE + REM
ROWS = 4 * SLOT
NPAD = 896
SHIFTS = (1, 3, 2)
OFFS = [(dxh, dy) for dxh in range(2) for dy in SHIFTS]
LATE_XL = ()
P1_EARLY = True
ORDER = ('P0', 'P1', 'P2', 'P3', 'P4', 'P5', 'X0', 'U00', 'E1', 'X1', 'X2', 'X3', 'X4', 'X5', 'U10', 'U20', 'E2', 'U30', 'U40', 'U50', 'M0', 'U01', 'L', 'H', 'U11', 'U21', 'U31', 'U41', 'U51', 'C', 'M1', 'M2', 'G', 'M3', 'M4', 'Q', 'M6', 'J', 'M5', 'R', 'M7')


def piece_start(q):
    return 192 * q + 16 * (q // 3)


def kernel(slots, owner, integrals, packed, sector, out,
           sendbuf, fin, win, win_full, stage, stage_full, irecv, arecv,
           x_buf, e1, e2, s_buf, st_buf, acc, l_buf, arem, sec_rows,
           w_sem, wf_sem, s1_send, s1_recv, own_sem, p1_send, p1_recv, full_send, full_recv,
           z_send, z_recv, z2_send, z2_recv, xl_send, xl_recv, ex_send, ex_recv, a_send, a_recv):
    r = lax.axis_index("row")
    c = lax.axis_index("col")
    z, xl = r // 2, r % 2
    xh, y, k = c // 8, (c // 2) % 4, c % 2

    def col(xh_, y_, k_):
        return xh_ * 8 + (y_ % 4) * 2 + k_

    def remote(src, dst, ssem, rsem_, row_, col_):
        return pltpu.make_async_remote_copy(src_ref=src, dst_ref=dst, send_sem=ssem, recv_sem=rsem_,
                                            device_id=(row_, col_), device_id_type=MESH)

    sends = []

    def send(cp):
        cp.start()
        sends.append(cp)

    mate = c + 1 - 2 * k
    cross_c = c + 8 - 16 * xh
    row_flip = z * 2 + 1 - xl

    dx = (k + xl) % 2
    p_xh = (xh + dx) % 2
    p_row = z * 2 + (xl + dx) % 2
    p_cols = [col(p_xh, y + dy, kk) for dy in SHIFTS for kk in range(2)]
    full_c = [mate, col(1 - xh, y, 0), col(1 - xh, y, 1), c]

    def window(start, width):
        first = jnp.minimum(start // 128, (12800 - width) // 128) * 128
        return pl.multiple_of(first, 128), start - first

    win_off, win_cp = [], []
    for n in range(6):
        w0, off = window(p_cols[n] * TILE + piece_start(z), 384)
        cp = pltpu.make_async_copy(integrals.at[:, pl.ds(w0, 384)], win.at[n], w_sem.at[n])
        cp.start()
        win_off.append(off)
        win_cp.append(cp)
    full_off, full_cp = [], []
    for f in range(4):
        w0, off = window(full_c[f] * TILE, 896)
        cp = pltpu.make_async_copy(integrals.at[:, pl.ds(w0, 896)], win_full.at[f], wf_sem.at[f])
        cp.start()
        full_off.append(off)
        full_cp.append(cp)

    me = r * 16 + c

    def pick(n, carry):
        sendbuf[n] = packed[slots[n]]
        return carry
    lax.fori_loop(0, 128, pick, 0, unroll=8)

    def give(d, carry):
        to = (me + d) % 128
        remote(sendbuf.at[to], fin.at[me], s1_send, s1_recv, to // 16, to % 16).start()
        return carry
    lax.fori_loop(1, 128, give, 0)
    own1 = pltpu.make_async_copy(sendbuf.at[me], fin.at[me], own_sem)
    own1.start()

    def turn_piece(read, off, store):
        i = lax.broadcasted_iota(jnp.int32, (256, 384), 0)
        lane = lax.broadcasted_iota(jnp.int32, (256, 384), 1)
        pick_rows = jnp.where((i < PIECE) & (lane == i + off), 1.0, 0.0).astype(BF)
        dims = (((1,), (1,)), ((), ()))
        main = lax.dot_general(pick_rows[:PIECE], read(0, MAIN), dims, preferred_element_type=F32)
        rest = lax.dot_general(read(MAIN, REM), pick_rows, dims, preferred_element_type=F32)
        store(main.astype(BF), rest.astype(BF))

    def into(ref, row0):
        def store(main, rest):
            ref[pl.ds(row0, PIECE), :] = main
            ref[pl.ds(row0 + PIECE, REM), pl.ds(0, 256)] = rest
            ref[pl.ds(row0 + PIECE, REM), pl.ds(256, 128)] = jnp.zeros((REM, 128), BF)
        return store

    zrow = pl.multiple_of(z * SLOT, 16)

    def send_p1():
        for n in range(6):
            send(remote(stage.at[n], irecv.at[c, pl.ds(zrow, SLOT), :], p1_send.at[n],
                        p1_recv.at[dx * 3 + n // 2], p_row, p_cols[n]))

    for n in range(6):
        win_cp[n].wait()
        turn_piece(lambda k0, kn: win[n, pl.ds(k0, kn), :], win_off[n], into(stage.at[n], 0))
    if P1_EARLY:
        send_p1()

    def turn_full(f, ref):
        full_cp[f].wait()

        def one(q, carry):
            at = full_off[f] + piece_start(q)
            lane0 = jnp.minimum(at // 128, 4) * 128
            turn_piece(lambda k0, kn: win_full[f, pl.ds(k0, kn), pl.ds(pl.multiple_of(lane0, 128), 384)],
                       at - lane0, into(ref, pl.multiple_of(q * SLOT, 16)))
            return carry
        lax.fori_loop(0, 4, one, 0)

    for f in (1, 2, 0):
        turn_full(f, stage_full.at[f])
        send(remote(stage_full.at[f], irecv.at[c], full_send.at[f],
                    full_recv.at[0] if f == 0 else full_recv.at[1 + k], r if f == 0 else row_flip, full_c[f]))

    def table(b, carry):
        j = lax.broadcasted_iota(jnp.int32, (128, NPAD), 0)
        col_i = lax.broadcasted_iota(jnp.int32, (128, NPAD), 1) - 50 * b
        e1[pl.ds(pl.multiple_of(b * 128, 128), 128), :] = jnp.where((j < 50) & (col_i == j), 1.0, 0.0).astype(BF)
        e2[pl.ds(pl.multiple_of(b * 128, 128), 128), :] = jnp.where(
            (j >= 50) & (j < 100) & (col_i == j - 50), 1.0, 0.0).astype(BF)
        return carry
    lax.fori_loop(0, 16, table, 0)
    s_buf[pl.ds(TILE, NPAD - TILE), :] = jnp.zeros((NPAD - TILE, NPAD), BF)

    def src_col(o, half):
        dxh, dy = OFFS[o]
        core = xl if half == 0 else 1 - xl
        return col(xh + dxh - 2 * xh * dxh, y + 4 - dy, core)

    up, down = ((z + 1) % 4) * 2 + xl, ((z + 3) % 4) * 2 + xl
    zrows = [pl.multiple_of(((z + d) % 4) * SLOT, 16) for d in range(4)]

    def i_slot(o, half, d):
        return irecv.at[src_col(o, half), pl.ds(zrows[d], SLOT), :]

    def i_wait(ref, sem):
        remote(ref, ref, p1_send.at[0], sem, r, c).wait_recv()

    def to_xl(o, d):
        ref = i_slot(o, 0, d)
        send(remote(ref, ref, xl_send.at[o, d], xl_recv.at[o, d], row_flip, c))

    def both_ways(o, half):
        ref = i_slot(o, half, 0)
        send(remote(ref, ref, z_send.at[o, half, 0], z_recv.at[o, half, 0], up, c))
        send(remote(ref, ref, z_send.at[o, half, 1], z_recv.at[o, half, 1], down, c))

    def share(o):
        i_wait(i_slot(o, 0, 0), p1_recv.at[o])
        to_xl(o, 0)
        both_ways(o, 0)

    def share_xl(o):
        i_wait(i_slot(o, 1, 0), xl_recv.at[o, 0])
        if o not in LATE_XL:
            both_ways(o, 1)

    def one_end(o, half):
        d = 3 if half == 0 else 1
        ref = i_slot(o, half, d)
        i_wait(ref, z_recv.at[o, half, half])
        send(remote(ref, ref, z2_send.at[o, half], z2_recv.at[o, half], up if half == 0 else down, c))
        if o in LATE_XL:
            to_xl(o, d)

    def other_end(o, half):
        d = 1 if half == 0 else 3
        i_wait(i_slot(o, half, d), z_recv.at[o, half, 1 - half])
        if o in LATE_XL:
            to_xl(o, d)

    def far_end(o, half):
        i_wait(i_slot(o, half, 2), z2_recv.at[o, half])
        if o in LATE_XL:
            to_xl(o, 2)

    def rest_of(o):
        if o in LATE_XL:
            for d in (1, 3, 2):
                i_wait(i_slot(o, 1, d), xl_recv.at[o, d])
        else:
            other_end(o, 0)
            far_end(o, 0)
            other_end(o, 1)
            far_end(o, 1)

    if not P1_EARLY:
        send_p1()
    turn_full(3, irecv.at[c])

    def line(first, count):
        at = first // 128
        parts = [sector[pl.ds(jnp.minimum(at + i, 49), 1), :] for i in range(count)]
        flat = jnp.broadcast_to(jnp.concatenate(parts, axis=1), (8, 128 * count))
        return pltpu.roll(flat, 128 * count - (first - at * 128), axis=1)
    sec_cols = line(r * TILE, 8)[0:1, :NPAD]
    sec_rows[...] = jnp.broadcast_to(line(c * KB, 5)[0:1, :512], (128, 512)).astype(F32).T
    sec_cols = sec_cols.astype(F32)

    own_half = s_buf.at[pl.ds(pl.multiple_of(k * KB, 16), KB), :]
    mate_half = s_buf.at[pl.ds(pl.multiple_of((1 - k) * KB, 16), KB), :]

    def assemble():
        own1.wait()
        remote(sendbuf.at[pl.ds(0, 127)], fin.at[pl.ds(0, 127)], s1_send, s1_recv, r, c).wait_recv()

        def put(a, carry):
            for b in range(16):
                x_buf[pl.ds(pl.multiple_of(32 * a, 32), 32), pl.ds(128 * b, 128)] = fin[owner[16 * a + b]]
            return carry
        lax.fori_loop(0, 8, put, 0)
        m_i = lax.broadcasted_iota(jnp.int32, (KB, 256), 0)
        n_i = lax.broadcasted_iota(jnp.int32, (KB, 256), 1)
        blk = (m_i * 1311) >> 16
        inner = m_i - 50 * blk
        f1 = jnp.where((inner < 32) & (n_i == 32 * blk + inner), 1.0, 0.0).astype(BF)
        f2 = jnp.where((inner >= 32) & (n_i == 32 * blk + inner - 32), 1.0, 0.0).astype(BF)
        for n0, nw, k0, kw in ((0, 256, 0, 768), (256, 256, 640, 768), (512, 256, 1280, 768), (768, 128, 1920, 128)):
            x = x_buf[:, pl.ds(k0, kw)]
            y1 = jnp.dot(x, e1[pl.ds(k0, kw), pl.ds(n0, nw)], preferred_element_type=F32).astype(BF)
            y2 = jnp.dot(x, e2[pl.ds(k0, kw), pl.ds(n0, nw)], preferred_element_type=F32).astype(BF)
            part = jnp.dot(f1, y1, preferred_element_type=F32) + jnp.dot(f2, y2, preferred_element_type=F32)
            s_buf[pl.ds(pl.multiple_of(k * KB, 16), KB), pl.ds(n0, nw)] = part.astype(BF)
        send(remote(own_half, own_half, ex_send.at[0], ex_recv.at[0], r, mate))

    yup, ydown = col(xh, y + 1, k), col(xh, y + 3, k)

    def a_send_to(cc, i, j, dest):
        send(remote(arecv.at[cc], arecv.at[cc], a_send.at[i], a_recv.at[j], r, dest))

    def a_wait(cc, j):
        remote(arecv.at[cc], arecv.at[cc], a_send.at[0], a_recv.at[j], r, c).wait_recv()

    def xy(dxh, dy, kk):
        return col(xh + dxh - 2 * xh * dxh, y + dy + 4, kk)

    def complete():
        remote(mate_half, mate_half, ex_send.at[0], ex_recv.at[0], r, c).wait_recv()

        def turn(i, carry):
            at = pl.ds(pl.multiple_of(i * 128, 128), 128)
            st_buf[:, at] = s_buf[at, pl.ds(pl.multiple_of(k * MAIN, 128), 512)].T
            return carry
        lax.fori_loop(0, 7, turn, 0)

        def choose(i, carry):
            row0 = pl.multiple_of(i * 80, 16)
            straight = s_buf[pl.ds(pl.multiple_of(k * KB + row0, 16), 80), :]
            flipped = st_buf[pl.ds(pl.multiple_of(16 * k + row0, 16), 80), :]
            g_k = lax.broadcasted_iota(jnp.int32, (80, NPAD), 0) + (c * KB + row0)
            g_n = lax.broadcasted_iota(jnp.int32, (80, NPAD), 1) + r * TILE
            tile = jnp.where(g_k <= g_n, straight.astype(F32), flipped.astype(F32))
            tile = jnp.where(sec_rows[pl.ds(row0, 80), 0:1] == sec_cols, tile, 0.0)
            arecv[c, pl.ds(row0, 80), :] = tile.astype(BF)
            return carry
        lax.fori_loop(0, 5, choose, 0)
        a_send_to(c, 0, 1, yup)
        a_send_to(c, 1, 2, ydown)
        a_send_to(c, 2, 0, cross_c)
        a_send_to(c, 3, 8, mate)

    def from_x():
        a_wait(cross_c, 0)
        a_send_to(cross_c, 4, 3, yup)
        a_send_to(cross_c, 5, 4, ydown)
        a_send_to(cross_c, 6, 9, mate)

    def from_y(dxh, dy, j, on, to_mate):
        cc = xy(dxh, dy, k)
        a_wait(cc, j)
        if on is not None:
            a_send_to(cc, *on)
        a_send_to(cc, *to_mate, mate)

    def product(dxh, dy, first):
        c0, c1 = xy(dxh, dy, 0), xy(dxh, dy, 1)

        def cut(n0, nw):
            at = pl.ds(n0, nw)
            left = jnp.concatenate([irecv[c0], irecv[c1]], axis=1)
            right = jnp.concatenate([arecv[c0, pl.ds(0, MAIN), at], arecv[c1, pl.ds(0, MAIN), at]], axis=0)
            part = jnp.dot(left, right, preferred_element_type=F32)
            if first:
                acc[:, at] = part
            else:
                acc[:, at] += part

        def step(i, carry):
            cut(pl.multiple_of(i * 256, 256), 256)
            return carry
        lax.fori_loop(0, 3, step, 0)
        cut(768, 128)

    def whole(cc, sem):
        ref = irecv.at[cc]
        remote(ref, ref, full_send.at[0], full_recv.at[sem], r, c).wait_recv()

    def multiply(i, first):
        dxh, dy, j = ((0, 0, 8), (1, 0, 9), (0, -1, 10), (0, 1, 11), (1, 1, 12), (1, -1, 13), (0, 2, 14), (1, 2, 15))[i]
        if i == 0:
            whole(mate, 0)
        elif i == 1:
            whole(xy(1, 0, 0), 1)
            whole(xy(1, 0, 1), 2)
        else:
            rest_of(dxh * 3 + {-1: 0, 1: 1, 2: 2}[dy])
        a_wait(xy(dxh, dy, 1 - k), j)
        product(dxh, dy, first)

    steps = {"E1": assemble, "E2": complete, "C": from_x}
    for o in range(6):
        steps["P%d" % o] = functools.partial(share, o)
        steps["X%d" % o] = functools.partial(share_xl, o)
        for half in range(2):
            steps["U%d%d" % (o, half)] = functools.partial(one_end, o, half)
            steps["V%d%d" % (o, half)] = functools.partial(other_end, o, half)
            steps["W%d%d" % (o, half)] = functools.partial(far_end, o, half)
    steps["L"] = functools.partial(from_y, 0, -1, 1, (7, 5, yup), (8, 10))
    steps["H"] = functools.partial(from_y, 0, 1, 2, None, (9, 11))
    steps["G"] = functools.partial(from_y, 1, 1, 4, (10, 6, ydown), (11, 12))
    steps["J"] = functools.partial(from_y, 1, -1, 3, None, (12, 13))
    steps["Q"] = functools.partial(from_y, 0, 2, 5, None, (13, 14))
    steps["R"] = functools.partial(from_y, 1, 2, 6, None, (14, 15))
    first = True
    for name in ORDER:
        if name[0] == "M":
            multiply(int(name[1:]), first)
            first = False
        else:
            steps[name]()

    for cc in range(16):
        arem[pl.ds(16 * cc, 16), :] = arecv[cc, pl.ds(MAIN, REM), :]
        for q in range(4):
            l_buf[q, pl.ds(16 * cc, 16), :] = irecv[cc, pl.ds(q * SLOT + PIECE, REM), pl.ds(0, 256)]
    for q, (skip, row0) in enumerate(((0, 0), (16, 208), (16, 400), (0, 592))):
        part = lax.dot_general(l_buf[q], arem[...], (((0,), (0,)), ((), ())), preferred_element_type=F32)
        rows = PIECE - skip
        total = acc[pl.ds(q * SLOT + skip, rows), pl.ds(0, TILE)] + part[skip:PIECE, :TILE]
        out[pl.ds(row0, rows), :] = total.astype(BF)

    for cp in sends:
        cp.wait_send()
    remote(sendbuf.at[pl.ds(0, 127)], fin.at[pl.ds(0, 127)], s1_send, s1_recv, r, c).wait_send()


def slot_table(owner_map, me):
    index = jnp.arange(128, dtype=jnp.int32)
    mine = jnp.sum(jnp.where(owner_map == me, index, 0))
    a, b = mine // 16, mine % 16
    rr, cc = index // 16, index % 16
    lo, hi, h = jnp.minimum(rr, cc // 2), jnp.maximum(rr, cc // 2), cc % 2
    e0 = (a > b).astype(jnp.int32)
    e1 = (a + 8 > b).astype(jnp.int32)
    down = 2 * lo + h
    before = 8 * down - (lo * (lo - 1) + lo * (e0 + e1) + h * (lo + e0))
    first = lo + jnp.where(h == 1, e1, e0)
    return jnp.clip(before + hi - first, 0, 71)


def body(integrals, packed_store, pair_sector, owner_map):
    r = lax.axis_index("row")
    c = lax.axis_index("col")
    slots = slot_table(owner_map, r * 16 + c)
    pad = jnp.zeros((72, 14, 50), BF)
    low = jnp.concatenate([packed_store[:, 32:, :], pad], axis=1)
    packed = jnp.concatenate([packed_store[:, :32, :], low, jnp.zeros((72, 32, 28), BF)], axis=2)
    dma = pltpu.SemaphoreType.DMA
    vm = lambda *s: pltpu.VMEM(s, BF)
    return pl.pallas_call(
        kernel,
        out_shape=jax.ShapeDtypeStruct((TILE, TILE), BF),
        in_specs=[pl.BlockSpec(memory_space=pltpu.SMEM)] * 2 + [pl.BlockSpec(memory_space=pl.ANY)]
        + [pl.BlockSpec(memory_space=pltpu.VMEM)] * 2,
        out_specs=pl.BlockSpec(memory_space=pltpu.VMEM),
        scratch_shapes=[
            vm(128, 32, 128), vm(128, 32, 128),
            vm(6, KB, 384), vm(4, KB, 896), vm(6, SLOT, MAIN), vm(3, ROWS, MAIN), vm(16, ROWS, MAIN), vm(16, KB, NPAD),
            vm(256, 2048), vm(2048, NPAD), vm(2048, NPAD), vm(NPAD, NPAD), vm(512, NPAD),
            pltpu.VMEM((ROWS, NPAD), F32), vm(4, 256, 256), vm(256, NPAD), pltpu.VMEM((512, 128), F32),
            dma((6,)), dma((4,)), dma, dma, dma,
            dma((6,)), dma((6,)), dma((3,)), dma((3,)),
            dma((6, 2, 2)), dma((6, 2, 2)), dma((6, 2)), dma((6, 2)), dma((6, 4)), dma((6, 4)), dma((1,)), dma((1,)),
            dma((15,)), dma((16,)),
        ],
        compiler_params=pltpu.CompilerParams(has_side_effects=True, vmem_limit_bytes=60 * 2**20),
        cost_estimate=pl.CostEstimate(flops=2 * 800 * 800 * 6400, bytes_accessed=20_000_000, transcendentals=0),
    )(slots, owner_map, integrals.T, packed, pair_sector.reshape(50, 128))


def solution(mesh):
    in_specs = (P(None, "col"), P(("row", "col"), None, None), P(), P())
    return jax.shard_map(body, mesh=mesh, in_specs=in_specs, out_specs=P("col", "row"), check_vma=False)
```

time: 157 us -> 132 us (0.84)
  the two profiles are of different devices: /device:TPU:1 before, /device:TPU:6 now
where the time goes in v2:
time: 132 us
  Pallas kernels  121 us (92%)
  local copies, waits for them, and re-layouts  4.89 us (4%)
  other arithmetic  3.1 us (2%)
  between operations  2.66 us (2%)
    pallas_call x1, Pallas kernels, body(): pl.pallas_call(kernel, out_shape=jax.ShapeDtypeStruct((TILE, TILE), BF),...  121 us
    unnamed x3, local copies, waits for them, and re-layouts  3.84 us

profile of v2, /device:TPU:6, one launch (start us, length us, event | category | flops | bytes accessed | tf_op | source)
XLA Modules:
  0.0 131.9 jit_solution(8718097286480138100)
XLA Ops:
  0.0 0.0 slice-start
  0.0 1.3 %fusion.4 = s32[]{:T(128)} fusion(s32[128]{0:T(128)} %owner.1, s32[]{:T(128)S(6)} %add.72), kind=kLoop, calls=%fused_computation.18 | loop fusion | flops 383 | bytes 520 | tf_op jit(solution)/shard_map/reduce_sum | solution.py:379
  4.0 0.5 fusion.8.slots
  4.5 0.1 pad.3.clone
  4.6 1.0 slice.7
  5.6 0.3 copy.8
  5.9 0.0 slice-done
  5.9 1.0 copy.7
  6.9 1.2 fusion.3.packed
  8.1 121.2 %shard_map.46 = bf16[800,800]{1,0:T(8,128)(2,1)} custom-call(s32[128]{0:T(128)} %fusion.8.slots, s32[128]{0:T(128)} %owner.1, bf16[400,12800]{1,0:T(8,128)(2,1)} %bitcast.2, bf16[72,32,128]{2,1,0:T(8,128)(2,1)} %fusion.3.packed, s32[50,128]{1,0:T(8,128)} %bitcast.3), custom_call_target="tpu_custom_call" | custom-call | flops 8192000000 | bytes 20000000 | tf_op jit(solution)/shard_map/pallas_call | solution.py:400
  129.3 2.6 %copy.10 = bf16[800,800]{1,0:T(8,128)(2,1)} copy(bf16[800,800]{1,0:T(8,128)(2,1)} %shard_map.46) | data formatting | bytes 2560000
  (1 shorter events, 0.0 us)
Async XLA Ops:
  0.0 5.9 %slice-start = ((bf16[72,50,50]{0,2,1:T(8,128)(2,1)}), bf16[72,32,50]{0,2,1:T(8,128)(2,1)S(1)}, s32[]{:S(2)}) async-start(bf16[72,50,50]{0,2,1:T(8,128)(2,1)} %param.5), calls=%async_computation | async-start | bytes 917504 | tf_op jit(solution)/shard_map/slice | solution.py:397

commit v3 on v2

--- a/solution.py
+++ b/solution.py
@@ -19,11 +19,16 @@
 SLOT = PIECE + REM
 ROWS = 4 * SLOT
 NPAD = 896
+NMAIN = 768
+NROWS = KB + 32
+WHOLE, LOW, HIGH = (0, NROWS), (0, 208), (208, 224)
+CUTS_X = ((0, 144), (144, 144), (288, 144))
+X_SEMS = ((2, 0), (17, 18), (18, 19))
 SHIFTS = (1, 3, 2)
 OFFS = [(dxh, dy) for dxh in range(2) for dy in SHIFTS]
-LATE_XL = ()
-P1_EARLY = True
-ORDER = ('P0', 'P1', 'P2', 'P3', 'P4', 'P5', 'X0', 'U00', 'E1', 'X1', 'X2', 'X3', 'X4', 'X5', 'U10', 'U20', 'E2', 'U30', 'U40', 'U50', 'M0', 'U01', 'L', 'H', 'U11', 'U21', 'U31', 'U41', 'U51', 'C', 'M1', 'M2', 'G', 'M3', 'M4', 'Q', 'M6', 'J', 'M5', 'R', 'M7')
+LATE_XL = (4, 5)
+EARLY = 2
+ORDER = ('F0', 'P0', 'Y0', 'ZA0', 'P3', 'Y3', 'P1', 'S2', 'P4', 'Y1', 'ZA3', 'ZA1', 'ZA4', 'E1', 'X0', 'Y4', 'ZB0', 'E2', 'X3', 'P2', 'P5', 'X1', 'ZB3', 'ZB1', 'ZA5', 'ZA2', 'U00', 'F', 'U30', 'M00', 'X4', 'U10', 'M01', 'V40', 'U40', 'M02', 'M03', 'L', 'H', 'U01', 'U31', 'U11', 'V50', 'C', 'Y5', 'Y2', 'Q', 'U50', 'U20', 'M20', 'X5', 'X2', 'ZB2', 'M21', 'W40', 'M22', 'M23', 'M30', 'M31', 'M32', 'J', 'G', 'M33', 'U21', 'M50', 'M51', 'M52', 'M53', 'M40', 'M41', 'M42', 'W50', 'M43', 'M10', 'M11', 'M12', 'R', 'M13', 'M60', 'M61', 'M62', 'M63', 'M70', 'M71', 'M72', 'M73')
 
 
 def piece_start(q):
@@ -32,7 +37,7 @@
 
 def kernel(slots, owner, integrals, packed, sector, out,
            sendbuf, fin, win, win_full, stage, stage_full, irecv, arecv,
-           x_buf, e1, e2, s_buf, st_buf, acc, l_buf, arem, sec_rows,
+           x_buf, e1, e2, s_buf, st_buf, acc, l_buf, arem, sec_rows, tail,
            w_sem, wf_sem, s1_send, s1_recv, own_sem, p1_send, p1_recv, full_send, full_recv,
            z_send, z_recv, z2_send, z2_recv, xl_send, xl_recv, ex_send, ex_recv, a_send, a_recv):
     r = lax.axis_index("row")
@@ -56,6 +61,17 @@
     mate = c + 1 - 2 * k
     cross_c = c + 8 - 16 * xh
     row_flip = z * 2 + 1 - xl
+
+    me = r * 16 + c
+    barrier = pltpu.get_barrier_semaphore()
+
+    def greet(dr, carry):
+        for dc in range(16):
+            pl.semaphore_signal(barrier, inc=1, device_id=((r + dr) % 8, (c + dc) % 16), device_id_type=MESH)
+        return carry
+    for dc in range(1, 16):
+        pl.semaphore_signal(barrier, inc=1, device_id=(r, (c + dc) % 16), device_id_type=MESH)
+    lax.fori_loop(1, 8, greet, 0)
 
     dx = (k + xl) % 2
     p_xh = (xh + dx) % 2
@@ -82,20 +98,10 @@
         full_off.append(off)
         full_cp.append(cp)
 
-    me = r * 16 + c
-
     def pick(n, carry):
         sendbuf[n] = packed[slots[n]]
         return carry
     lax.fori_loop(0, 128, pick, 0, unroll=8)
-
-    def give(d, carry):
-        to = (me + d) % 128
-        remote(sendbuf.at[to], fin.at[me], s1_send, s1_recv, to // 16, to % 16).start()
-        return carry
-    lax.fori_loop(1, 128, give, 0)
-    own1 = pltpu.make_async_copy(sendbuf.at[me], fin.at[me], own_sem)
-    own1.start()
 
     def turn_piece(read, off, store):
         i = lax.broadcasted_iota(jnp.int32, (256, 384), 0)
@@ -115,16 +121,35 @@
 
     zrow = pl.multiple_of(z * SLOT, 16)
 
-    def send_p1():
-        for n in range(6):
-            send(remote(stage.at[n], irecv.at[c, pl.ds(zrow, SLOT), :], p1_send.at[n],
-                        p1_recv.at[dx * 3 + n // 2], p_row, p_cols[n]))
-
-    for n in range(6):
+    def send_p1(i):
+        for n in (2 * i, 2 * i + 1):
+            send(remote(stage.at[n], irecv.at[c, pl.ds(zrow, SLOT), :], p1_send.at[n], p1_recv.at[dx * 3 + i], p_row, p_cols[n]))
+
+    def stage_p1(n):
         win_cp[n].wait()
         turn_piece(lambda k0, kn: win[n, pl.ds(k0, kn), :], win_off[n], into(stage.at[n], 0))
-    if P1_EARLY:
-        send_p1()
+
+    for n in range(2 * EARLY):
+        stage_p1(n)
+    pl.semaphore_wait(barrier, 127)
+    for i in range(EARLY):
+        send_p1(i)
+
+    def give(to_r, to_c):
+        to = to_r * 16 + to_c
+        remote(sendbuf.at[to], fin.at[me], s1_send, s1_recv, to_r, to_c).start()
+
+    def give_row(d, carry):
+        for dc in range(16):
+            give((r + d) % 8, (c + dc) % 16)
+        return carry
+    for dc in range(1, 16):
+        give(r, (c + dc) % 16)
+    lax.fori_loop(1, 8, give_row, 0)
+    own1 = pltpu.make_async_copy(sendbuf.at[me], fin.at[me], own_sem)
+    own1.start()
+    for n in range(2 * EARLY, 6):
+        stage_p1(n)
 
     def turn_full(f, ref):
         full_cp[f].wait()
@@ -137,10 +162,20 @@
             return carry
         lax.fori_loop(0, 4, one, 0)
 
-    for f in (1, 2, 0):
-        turn_full(f, stage_full.at[f])
+    def send_full(f):
         send(remote(stage_full.at[f], irecv.at[c], full_send.at[f],
                     full_recv.at[0] if f == 0 else full_recv.at[1 + k], r if f == 0 else row_flip, full_c[f]))
+
+    def send_fulls():
+        send_full(1)
+        send_full(2)
+
+    def prepare():
+        for f in range(3):
+            turn_full(f, stage_full.at[f])
+        send_full(0)
+        turn_full(3, irecv.at[c])
+        lax.fori_loop(0, 16, table, 0)
 
     def table(b, carry):
         j = lax.broadcasted_iota(jnp.int32, (128, NPAD), 0)
@@ -149,7 +184,7 @@
         e2[pl.ds(pl.multiple_of(b * 128, 128), 128), :] = jnp.where(
             (j >= 50) & (j < 100) & (col_i == j - 50), 1.0, 0.0).astype(BF)
         return carry
-    lax.fori_loop(0, 16, table, 0)
+    tail[pl.ds(KB, 112), :] = jnp.zeros((112, 128), F32)
     s_buf[pl.ds(TILE, NPAD - TILE), :] = jnp.zeros((NPAD - TILE, NPAD), BF)
 
     def src_col(o, half):
@@ -175,15 +210,11 @@
         send(remote(ref, ref, z_send.at[o, half, 0], z_recv.at[o, half, 0], up, c))
         send(remote(ref, ref, z_send.at[o, half, 1], z_recv.at[o, half, 1], down, c))
 
-    def share(o):
+    def shared(o):
         i_wait(i_slot(o, 0, 0), p1_recv.at[o])
-        to_xl(o, 0)
-        both_ways(o, 0)
-
-    def share_xl(o):
+
+    def shared_xl(o):
         i_wait(i_slot(o, 1, 0), xl_recv.at[o, 0])
-        if o not in LATE_XL:
-            both_ways(o, 1)
 
     def one_end(o, half):
         d = 3 if half == 0 else 1
@@ -213,10 +244,6 @@
             far_end(o, 0)
             other_end(o, 1)
             far_end(o, 1)
-
-    if not P1_EARLY:
-        send_p1()
-    turn_full(3, irecv.at[c])
 
     def line(first, count):
         at = first // 128
@@ -255,11 +282,16 @@
 
     yup, ydown = col(xh, y + 1, k), col(xh, y + 3, k)
 
-    def a_send_to(cc, i, j, dest):
-        send(remote(arecv.at[cc], arecv.at[cc], a_send.at[i], a_recv.at[j], r, dest))
-
-    def a_wait(cc, j):
-        remote(arecv.at[cc], arecv.at[cc], a_send.at[0], a_recv.at[j], r, c).wait_recv()
+    def a_rows(cc, rows):
+        return arecv.at[cc, pl.ds(rows[0], rows[1]), :]
+
+    def a_send_to(cc, i, j, dest, rows=WHOLE):
+        ref = a_rows(cc, rows)
+        send(remote(ref, ref, a_send.at[i], a_recv.at[j], r, dest))
+
+    def a_wait(cc, j, rows=WHOLE):
+        ref = a_rows(cc, rows)
+        remote(ref, ref, a_send.at[0], a_recv.at[j], r, c).wait_recv()
 
     def xy(dxh, dy, kk):
         return col(xh + dxh - 2 * xh * dxh, y + dy + 4, kk)
@@ -281,16 +313,22 @@
             g_n = lax.broadcasted_iota(jnp.int32, (80, NPAD), 1) + r * TILE
             tile = jnp.where(g_k <= g_n, straight.astype(F32), flipped.astype(F32))
             tile = jnp.where(sec_rows[pl.ds(row0, 80), 0:1] == sec_cols, tile, 0.0)
-            arecv[c, pl.ds(row0, 80), :] = tile.astype(BF)
+            arecv[c, pl.ds(row0, 80), :] = tile[:, :NMAIN].astype(BF)
+            tail[pl.ds(row0, 80), :] = tile[:, NMAIN:]
             return carry
         lax.fori_loop(0, 5, choose, 0)
+        arecv[c, pl.ds(KB, 32), pl.ds(0, 512)] = tail[...].T[:32].astype(BF)
+        arecv[c, pl.ds(KB, 32), pl.ds(512, 256)] = jnp.zeros((32, 256), BF)
+        arecv[c, pl.ds(KB, 16), pl.ds(512, 128)] = tail[pl.ds(MAIN, 16), :].astype(BF)
+        for i, rows in enumerate(CUTS_X):
+            a_send_to(c, X_SEMS[i][0], X_SEMS[i][1], cross_c, rows=rows)
         a_send_to(c, 0, 1, yup)
         a_send_to(c, 1, 2, ydown)
-        a_send_to(c, 2, 0, cross_c)
         a_send_to(c, 3, 8, mate)
 
     def from_x():
-        a_wait(cross_c, 0)
+        for i, rows in enumerate(CUTS_X):
+            a_wait(cross_c, X_SEMS[i][1], rows)
         a_send_to(cross_c, 4, 3, yup)
         a_send_to(cross_c, 5, 4, ydown)
         a_send_to(cross_c, 6, 9, mate)
@@ -298,35 +336,44 @@
     def from_y(dxh, dy, j, on, to_mate):
         cc = xy(dxh, dy, k)
         a_wait(cc, j)
-        if on is not None:
-            a_send_to(cc, *on)
+        i, j2, dest, rows = on
+        a_send_to(cc, i, j2, dest, rows=rows)
         a_send_to(cc, *to_mate, mate)
 
-    def product(dxh, dy, first):
+    def from_y2(dxh, low, high, to_mate):
+        cc = xy(dxh, 2, k)
+        a_wait(cc, low, LOW)
+        a_wait(cc, high, HIGH)
+        a_send_to(cc, *to_mate, mate)
+
+    def product(dxh, dy, n, first):
         c0, c1 = xy(dxh, dy, 0), xy(dxh, dy, 1)
 
-        def cut(n0, nw):
-            at = pl.ds(n0, nw)
-            left = jnp.concatenate([irecv[c0], irecv[c1]], axis=1)
-            right = jnp.concatenate([arecv[c0, pl.ds(0, MAIN), at], arecv[c1, pl.ds(0, MAIN), at]], axis=0)
-            part = jnp.dot(left, right, preferred_element_type=F32)
+        def add(at, part):
             if first:
                 acc[:, at] = part
             else:
                 acc[:, at] += part
 
-        def step(i, carry):
-            cut(pl.multiple_of(i * 256, 256), 256)
-            return carry
-        lax.fori_loop(0, 3, step, 0)
-        cut(768, 128)
+        left = jnp.concatenate([irecv[c0], irecv[c1]], axis=1)
+        if n < 3:
+            at = pl.ds(n * 256, 256)
+            right = jnp.concatenate([arecv[c0, pl.ds(0, MAIN), at], arecv[c1, pl.ds(0, MAIN), at]], axis=0)
+            add(at, jnp.dot(left, right, preferred_element_type=F32))
+        else:
+            side = pl.ds(KB, 32)
+            right = jnp.concatenate([arecv[c0, side, pl.ds(0, MAIN)], arecv[c1, side, pl.ds(0, MAIN)]], axis=1)
+            add(pl.ds(NMAIN, 32), lax.dot_general(left, right, (((1,), (1,)), ((), ())), preferred_element_type=F32))
 
     def whole(cc, sem):
         ref = irecv.at[cc]
         remote(ref, ref, full_send.at[0], full_recv.at[sem], r, c).wait_recv()
 
-    def multiply(i, first):
+    def multiply(i, n, first):
         dxh, dy, j = ((0, 0, 8), (1, 0, 9), (0, -1, 10), (0, 1, 11), (1, 1, 12), (1, -1, 13), (0, 2, 14), (1, 2, 15))[i]
+        if n > 0:
+            product(dxh, dy, n, first)
+            return
         if i == 0:
             whole(mate, 0)
         elif i == 1:
@@ -335,32 +382,36 @@
         else:
             rest_of(dxh * 3 + {-1: 0, 1: 1, 2: 2}[dy])
         a_wait(xy(dxh, dy, 1 - k), j)
-        product(dxh, dy, first)
-
-    steps = {"E1": assemble, "E2": complete, "C": from_x}
+        product(dxh, dy, n, first)
+
+    steps = {"F": send_fulls, "F0": prepare, "E1": assemble, "E2": complete, "C": from_x}
+    for i in range(3):
+        steps["S%d" % i] = functools.partial(send_p1, i)
     for o in range(6):
-        steps["P%d" % o] = functools.partial(share, o)
-        steps["X%d" % o] = functools.partial(share_xl, o)
+        steps["P%d" % o] = functools.partial(shared, o)
+        steps["X%d" % o] = functools.partial(shared_xl, o)
+        steps["Y%d" % o] = functools.partial(to_xl, o, 0)
+        steps["ZA%d" % o] = functools.partial(both_ways, o, 0)
+        steps["ZB%d" % o] = functools.partial(both_ways, o, 1)
         for half in range(2):
             steps["U%d%d" % (o, half)] = functools.partial(one_end, o, half)
             steps["V%d%d" % (o, half)] = functools.partial(other_end, o, half)
             steps["W%d%d" % (o, half)] = functools.partial(far_end, o, half)
-    steps["L"] = functools.partial(from_y, 0, -1, 1, (7, 5, yup), (8, 10))
-    steps["H"] = functools.partial(from_y, 0, 1, 2, None, (9, 11))
-    steps["G"] = functools.partial(from_y, 1, 1, 4, (10, 6, ydown), (11, 12))
-    steps["J"] = functools.partial(from_y, 1, -1, 3, None, (12, 13))
-    steps["Q"] = functools.partial(from_y, 0, 2, 5, None, (13, 14))
-    steps["R"] = functools.partial(from_y, 1, 2, 6, None, (14, 15))
-    first = True
+    steps["L"] = functools.partial(from_y, 0, -1, 1, (7, 5, yup, LOW), (8, 10))
+    steps["H"] = functools.partial(from_y, 0, 1, 2, (15, 16, ydown, HIGH), (9, 11))
+    steps["G"] = functools.partial(from_y, 1, 1, 4, (10, 6, ydown, HIGH), (11, 12))
+    steps["J"] = functools.partial(from_y, 1, -1, 3, (16, 17, yup, LOW), (12, 13))
+    steps["Q"] = functools.partial(from_y2, 0, 5, 16, (13, 14))
+    steps["R"] = functools.partial(from_y2, 1, 17, 6, (14, 15))
     for name in ORDER:
         if name[0] == "M":
-            multiply(int(name[1:]), first)
-            first = False
+            multiply(int(name[1]), int(name[2]), name[1] == "0")
         else:
             steps[name]()
 
     for cc in range(16):
-        arem[pl.ds(16 * cc, 16), :] = arecv[cc, pl.ds(MAIN, REM), :]
+        arem[pl.ds(16 * cc, 16), pl.ds(0, NMAIN)] = arecv[cc, pl.ds(MAIN, REM), :]
+        arem[pl.ds(16 * cc, 16), pl.ds(NMAIN, 128)] = arecv[cc, pl.ds(KB, 16), pl.ds(512, 128)]
         for q in range(4):
             l_buf[q, pl.ds(16 * cc, 16), :] = irecv[cc, pl.ds(q * SLOT + PIECE, REM), pl.ds(0, 256)]
     for q, (skip, row0) in enumerate(((0, 0), (16, 208), (16, 400), (0, 592))):
@@ -389,9 +440,7 @@
 
 
 def body(integrals, packed_store, pair_sector, owner_map):
-    r = lax.axis_index("row")
-    c = lax.axis_index("col")
-    slots = slot_table(owner_map, r * 16 + c)
+    slots = slot_table(owner_map, lax.axis_index("row") * 16 + lax.axis_index("col"))
     pad = jnp.zeros((72, 14, 50), BF)
     low = jnp.concatenate([packed_store[:, 32:, :], pad], axis=1)
     packed = jnp.concatenate([packed_store[:, :32, :], low, jnp.zeros((72, 32, 28), BF)], axis=2)
@@ -405,15 +454,15 @@
         out_specs=pl.BlockSpec(memory_space=pltpu.VMEM),
         scratch_shapes=[
             vm(128, 32, 128), vm(128, 32, 128),
-            vm(6, KB, 384), vm(4, KB, 896), vm(6, SLOT, MAIN), vm(3, ROWS, MAIN), vm(16, ROWS, MAIN), vm(16, KB, NPAD),
+            vm(6, KB, 384), vm(4, KB, 896), vm(6, SLOT, MAIN), vm(3, ROWS, MAIN), vm(16, ROWS, MAIN), vm(16, NROWS, NMAIN),
             vm(256, 2048), vm(2048, NPAD), vm(2048, NPAD), vm(NPAD, NPAD), vm(512, NPAD),
-            pltpu.VMEM((ROWS, NPAD), F32), vm(4, 256, 256), vm(256, NPAD), pltpu.VMEM((512, 128), F32),
+            pltpu.VMEM((ROWS, NPAD), F32), vm(4, 256, 256), vm(256, NPAD), pltpu.VMEM((512, 128), F32), pltpu.VMEM((512, 128), F32),
             dma((6,)), dma((4,)), dma, dma, dma,
             dma((6,)), dma((6,)), dma((3,)), dma((3,)),
             dma((6, 2, 2)), dma((6, 2, 2)), dma((6, 2)), dma((6, 2)), dma((6, 4)), dma((6, 4)), dma((1,)), dma((1,)),
-            dma((15,)), dma((16,)),
+            dma((19,)), dma((20,)),
         ],
-        compiler_params=pltpu.CompilerParams(has_side_effects=True, vmem_limit_bytes=60 * 2**20),
+        compiler_params=pltpu.CompilerParams(collective_id=1, has_side_effects=True, vmem_limit_bytes=60 * 2**20),
         cost_estimate=pl.CostEstimate(flops=2 * 800 * 800 * 6400, bytes_accessed=20_000_000, transcendentals=0),
     )(slots, owner_map, integrals.T, packed, pair_sector.reshape(50, 128))
 

time: 132 us -> 110 us (0.83)
  the two profiles are of different devices: /device:TPU:6 before, /device:TPU:1 now
where the time goes in v3:
time: 110 us
  Pallas kernels  99.4 us (90%)
  local copies, waits for them, and re-layouts  4.89 us (4%)
  other arithmetic  3.1 us (3%)
  between operations  2.66 us (2%)
    pallas_call x1, Pallas kernels, body(): pl.pallas_call(kernel, out_shape=jax.ShapeDtypeStruct((TILE, TILE), BF),...  99.4 us
    unnamed x3, local copies, waits for them, and re-layouts  3.84 us

profile of v3, /device:TPU:1, one launch (start us, length us, event | category | flops | bytes accessed | tf_op | source)
XLA Modules:
  0.0 110.1 jit_solution(4757581514537463599)
XLA Ops:
  0.0 0.0 slice-start
  0.0 1.3 %fusion.4 = s32[]{:T(128)} fusion(s32[128]{0:T(128)} %owner.1, s32[]{:T(128)S(6)} %add.72), kind=kLoop, calls=%fused_computation.18 | loop fusion | flops 383 | bytes 520 | tf_op jit(solution)/shard_map/reduce_sum | solution.py:430
  4.0 0.5 fusion.8.slots
  4.5 0.1 pad.3.clone
  4.6 1.0 slice.7
  5.6 0.3 copy.8
  5.9 0.0 slice-done
  5.9 1.0 copy.7
  6.9 1.2 %fusion.3.packed = bf16[72,32,128]{2,1,0:T(8,128)(2,1)} fusion(bf16[72,18,50]{2,1,0:T(8,128)(2,1)S(1)} %copy.8, bf16[72,32,50]{2,1,0:T(8,128)(2,1)S(1)} %copy.7, bf16[128]{0:T(256)(128)(2,1)S(1)} %pad.3.clone), kind=kLoop, calls=%fused_computation.5 | loop fusion | flops 2949120 | bytes 950080 | tf_op jit(solution)/shard_map/concatenate | solution.py:446
  8.1 99.4 %shard_map.46 = bf16[800,800]{1,0:T(8,128)(2,1)} custom-call(s32[128]{0:T(128)} %fusion.8.slots, s32[128]{0:T(128)} %owner.1, bf16[400,12800]{1,0:T(8,128)(2,1)} %bitcast.2, bf16[72,32,128]{2,1,0:T(8,128)(2,1)} %fusion.3.packed, s32[50,128]{1,0:T(8,128)} %bitcast.3), custom_call_target="tpu_custom_call" | custom-call | flops 8192000000 | bytes 20000000 | tf_op jit(solution)/shard_map/pallas_call | solution.py:449
  107.5 2.6 %copy.10 = bf16[800,800]{1,0:T(8,128)(2,1)} copy(bf16[800,800]{1,0:T(8,128)(2,1)} %shard_map.46) | data formatting | bytes 2560000
  (1 shorter events, 0.0 us)
Async XLA Ops:
  0.0 5.9 %slice-start = ((bf16[72,50,50]{0,2,1:T(8,128)(2,1)}), bf16[72,32,50]{0,2,1:T(8,128)(2,1)S(1)}, s32[]{:S(2)}) async-start(bf16[72,50,50]{0,2,1:T(8,128)(2,1)} %param.5), calls=%async_computation | async-start | bytes 917504 | tf_op jit(solution)/shard_map/slice | solution.py:446

commit v4 on v3

--- a/solution.py
+++ b/solution.py
@@ -2,6 +2,7 @@
 
 import jax
 import jax.numpy as jnp
+import numpy as np
 from jax import lax
 from jax.experimental import pallas as pl
 from jax.experimental.pallas import tpu as pltpu
@@ -425,18 +426,21 @@
     remote(sendbuf.at[pl.ds(0, 127)], fin.at[pl.ds(0, 127)], s1_send, s1_recv, r, c).wait_send()
 
 
+def slot_constants():
+    table = np.zeros((128, 128), np.int32)
+    for cls in range(128):
+        a, b = cls // 16, cls % 16
+        blocks = [(a + 8 * t, b + 16 * u) for t in range(16) for u in range(8) if a + 8 * t <= b + 16 * u]
+        place = {block: i for i, block in enumerate(blocks)}
+        for n in range(128):
+            rr, cc = n // 16, n % 16
+            lo, hi, h = min(rr, cc // 2), max(rr, cc // 2), cc % 2
+            table[cls, n] = place.get((a + 8 * (2 * lo + h), b + 16 * hi), 0)
+    return table
+
+
 def slot_table(owner_map, me):
-    index = jnp.arange(128, dtype=jnp.int32)
-    mine = jnp.sum(jnp.where(owner_map == me, index, 0))
-    a, b = mine // 16, mine % 16
-    rr, cc = index // 16, index % 16
-    lo, hi, h = jnp.minimum(rr, cc // 2), jnp.maximum(rr, cc // 2), cc % 2
-    e0 = (a > b).astype(jnp.int32)
-    e1 = (a + 8 > b).astype(jnp.int32)
-    down = 2 * lo + h
-    before = 8 * down - (lo * (lo - 1) + lo * (e0 + e1) + h * (lo + e0))
-    first = lo + jnp.where(h == 1, e1, e0)
-    return jnp.clip(before + hi - first, 0, 71)
+    return jnp.sum(jnp.where((owner_map == me)[:, None], jnp.asarray(slot_constants()), 0), axis=0)
 
 
 def body(integrals, packed_store, pair_sector, owner_map):

time: 110 us -> 108 us (0.982)
  between operations: 2.66 us -> 0.04 us
where the time goes in v4:
time: 108 us
  Pallas kernels  99.4 us (92%)
  local copies, waits for them, and re-layouts  4.89 us (5%)
  other arithmetic  3.39 us (3%)
    pallas_call x1, Pallas kernels, body(): pl.pallas_call(kernel, out_shape=jax.ShapeDtypeStruct((TILE, TILE), BF),...  99.4 us
    unnamed x3, local copies, waits for them, and re-layouts  3.84 us

profile of v4, /device:TPU:1, one launch (start us, length us, event | category | flops | bytes accessed | tf_op | source)
XLA Modules:
  0.0 107.7 jit_solution(10129528485397499427)
XLA Ops:
  0.0 0.0 slice-start
  0.0 0.7 broadcast_compare_fusion
  0.7 1.5 %select_reduce_fusion.slots = s32[128]{0:T(128)} fusion(s32[128,128]{1,0:T(8,128)} %constant.18.clone, pred[128]{0:T(512)(128)(4,1)S(1)} %broadcast_compare_fusion), kind=kLoop, calls=%fused_computation.6 | loop fusion | flops 32640 | bytes 66176 | tf_op jit(solution)/shard_map/reduce_sum | solution.py:443
  2.2 0.1 pad.3.clone
  2.3 1.0 slice.7
  3.2 0.3 copy.11
  3.6 0.0 slice-done
  3.6 1.0 copy.10
  4.5 1.2 %fusion.3.packed = bf16[72,32,128]{2,1,0:T(8,128)(2,1)} fusion(bf16[72,18,50]{2,1,0:T(8,128)(2,1)S(1)} %copy.11, bf16[72,32,50]{2,1,0:T(8,128)(2,1)S(1)} %copy.10, bf16[128]{0:T(256)(128)(2,1)S(1)} %pad.3.clone), kind=kLoop, calls=%fused_computation.5 | loop fusion | flops 2949120 | bytes 950080 | tf_op jit(solution)/shard_map/concatenate | solution.py:450
  5.7 99.4 %shard_map.55 = bf16[800,800]{1,0:T(8,128)(2,1)} custom-call(s32[128]{0:T(128)} %select_reduce_fusion.slots, s32[128]{0:T(128)} %owner.1, bf16[400,12800]{1,0:T(8,128)(2,1)} %bitcast.2, bf16[72,32,128]{2,1,0:T(8,128)(2,1)} %fusion.3.packed, s32[50,128]{1,0:T(8,128)} %bitcast.3), custom_call_target="tpu_custom_call" | custom-call | flops 8192000000 | bytes 20000000 | tf_op jit(solution)/shard_map/pallas_call | solution.py:453
  105.2 2.6 %copy.13 = bf16[800,800]{1,0:T(8,128)(2,1)} copy(bf16[800,800]{1,0:T(8,128)(2,1)} %shard_map.55) | data formatting | bytes 2560000
  (1 shorter events, 0.0 us)
Async XLA Ops:
  0.0 3.6 %slice-start = ((bf16[72,50,50]{0,2,1:T(8,128)(2,1)}), bf16[72,32,50]{0,2,1:T(8,128)(2,1)S(1)}, s32[]{:S(2)}) async-start(bf16[72,50,50]{0,2,1:T(8,128)(2,1)} %param.6), calls=%async_computation | async-start | bytes 917504 | tf_op jit(solution)/shard_map/slice | solution.py:450

commit v5 on v4

--- a/solution.py
+++ b/solution.py
@@ -445,9 +445,8 @@
 
 def body(integrals, packed_store, pair_sector, owner_map):
     slots = slot_table(owner_map, lax.axis_index("row") * 16 + lax.axis_index("col"))
-    pad = jnp.zeros((72, 14, 50), BF)
-    low = jnp.concatenate([packed_store[:, 32:, :], pad], axis=1)
-    packed = jnp.concatenate([packed_store[:, :32, :], low, jnp.zeros((72, 32, 28), BF)], axis=2)
+    packed = (jnp.pad(packed_store[:, :32], ((0, 0), (0, 0), (0, 78)))
+              + jnp.pad(packed_store[:, 32:], ((0, 0), (0, 14), (50, 28))))
     dma = pltpu.SemaphoreType.DMA
     vm = lambda *s: pltpu.VMEM(s, BF)
     return pl.pallas_call(

time: 108 us -> 108 us (level)
    concatenate x1 -> x0, other arithmetic: 1.21 us -> none  [body(): jnp.concatenate([packed_store[:, :32, :], low, jnp.zeros((72, 32, 28), BF...]
where the time goes in v5:
time: 108 us
  Pallas kernels  99.4 us (92%)
  local copies, waits for them, and re-layouts  4.81 us (4%)
  other arithmetic  3.25 us (3%)
    pallas_call x1, Pallas kernels, body(): pl.pallas_call(kernel, out_shape=jax.ShapeDtypeStruct((TILE, TILE), BF),...  99.4 us
    unnamed x3, local copies, waits for them, and re-layouts  3.84 us

profile of v5, /device:TPU:1, one launch (start us, length us, event | category | flops | bytes accessed | tf_op | source)
XLA Modules:
  0.0 107.5 jit_solution(12674099600372244140)
XLA Ops:
  0.0 0.0 slice-start
  0.0 0.7 broadcast_compare_fusion
  0.7 1.5 %select_reduce_fusion.slots = s32[128]{0:T(128)} fusion(s32[128,128]{1,0:T(8,128)} %constant.17.clone, pred[128]{0:T(512)(128)(4,1)S(1)} %broadcast_compare_fusion), kind=kLoop, calls=%fused_computation.1 | loop fusion | flops 32640 | bytes 66176 | tf_op jit(solution)/shard_map/reduce_sum | solution.py:443
  2.2 1.0 slice.7
  3.2 0.3 copy.11
  3.5 0.0 slice-done
  3.5 1.0 copy.10
  4.5 1.1 pad_add_fusion.packed
  5.5 99.4 %shard_map.55 = bf16[800,800]{1,0:T(8,128)(2,1)} custom-call(s32[128]{0:T(128)} %select_reduce_fusion.slots, s32[128]{0:T(128)} %owner.1, bf16[400,12800]{1,0:T(8,128)(2,1)} %bitcast.2, bf16[72,32,128]{2,1,0:T(8,128)(2,1)} %pad_add_fusion.packed, s32[50,128]{1,0:T(8,128)} %bitcast.3), custom_call_target="tpu_custom_call" | custom-call | flops 8192000000 | bytes 20000000 | tf_op jit(solution)/shard_map/pallas_call | solution.py:452
  105.0 2.6 %copy.13 = bf16[800,800]{1,0:T(8,128)(2,1)} copy(bf16[800,800]{1,0:T(8,128)(2,1)} %shard_map.55) | data formatting | bytes 2560000
Async XLA Ops:
  0.0 3.5 %slice-start = ((bf16[72,50,50]{0,2,1:T(8,128)(2,1)}), bf16[72,32,50]{0,2,1:T(8,128)(2,1)S(1)}, s32[]{:S(2)}) async-start(bf16[72,50,50]{0,2,1:T(8,128)(2,1)} %param.6), calls=%async_computation | async-start | bytes 917504 | tf_op jit(solution)/shard_map/slice | solution.py:448

commit v6 on v5

--- a/solution.py
+++ b/solution.py
@@ -27,9 +27,9 @@
 X_SEMS = ((2, 0), (17, 18), (18, 19))
 SHIFTS = (1, 3, 2)
 OFFS = [(dxh, dy) for dxh in range(2) for dy in SHIFTS]
-LATE_XL = (4, 5)
+LATE_XL = (4,)
 EARLY = 2
-ORDER = ('F0', 'P0', 'Y0', 'ZA0', 'P3', 'Y3', 'P1', 'S2', 'P4', 'Y1', 'ZA3', 'ZA1', 'ZA4', 'E1', 'X0', 'Y4', 'ZB0', 'E2', 'X3', 'P2', 'P5', 'X1', 'ZB3', 'ZB1', 'ZA5', 'ZA2', 'U00', 'F', 'U30', 'M00', 'X4', 'U10', 'M01', 'V40', 'U40', 'M02', 'M03', 'L', 'H', 'U01', 'U31', 'U11', 'V50', 'C', 'Y5', 'Y2', 'Q', 'U50', 'U20', 'M20', 'X5', 'X2', 'ZB2', 'M21', 'W40', 'M22', 'M23', 'M30', 'M31', 'M32', 'J', 'G', 'M33', 'U21', 'M50', 'M51', 'M52', 'M53', 'M40', 'M41', 'M42', 'W50', 'M43', 'M10', 'M11', 'M12', 'R', 'M13', 'M60', 'M61', 'M62', 'M63', 'M70', 'M71', 'M72', 'M73')
+ORDER = ('F0', 'P0', 'Y0', 'ZA0', 'P3', 'ZA3', 'P1', 'ZA1', 'P4', 'ZA4', 'X0', 'Y3', 'ZB0', 'E1', 'S2', 'X3', 'Y1', 'E2', 'F', 'M00', 'M01', 'M02', 'U00', 'ZB3', 'U30', 'P2', 'ZA2', 'P5', 'U10', 'ZA5', 'X1', 'Y2', 'V40', 'U40', 'ZB1', 'U01', 'M03', 'L', 'H', 'U31', 'C', 'U11', 'X2', 'Y5', 'ZB2', 'Q', 'X5', 'Y4', 'ZB5', 'M20', 'M21', 'M22', 'M23', 'U20', 'U50', 'W40', 'U21', 'X4', 'M30', 'M31', 'M32', 'M33', 'U51', 'J', 'G', 'M50', 'M51', 'M52', 'M53', 'M40', 'M41', 'M42', 'M43', 'M10', 'M11', 'M12', 'M13', 'R', 'M60', 'M61', 'M62', 'M63', 'M70', 'M71', 'M72', 'M73')
 
 
 def piece_start(q):
@@ -39,7 +39,7 @@
 def kernel(slots, owner, integrals, packed, sector, out,
            sendbuf, fin, win, win_full, stage, stage_full, irecv, arecv,
            x_buf, e1, e2, s_buf, st_buf, acc, l_buf, arem, sec_rows, tail,
-           w_sem, wf_sem, s1_send, s1_recv, own_sem, p1_send, p1_recv, full_send, full_recv,
+           all_sem, w_sem, wf_sem, s1_send, s1_recv, own_sem, p1_send, p1_recv, full_send, full_recv,
            z_send, z_recv, z2_send, z2_recv, xl_send, xl_recv, ex_send, ex_recv, a_send, a_recv):
     r = lax.axis_index("row")
     c = lax.axis_index("col")
@@ -66,13 +66,15 @@
     me = r * 16 + c
     barrier = pltpu.get_barrier_semaphore()
 
-    def greet(dr, carry):
-        for dc in range(16):
-            pl.semaphore_signal(barrier, inc=1, device_id=((r + dr) % 8, (c + dc) % 16), device_id_type=MESH)
-        return carry
-    for dc in range(1, 16):
-        pl.semaphore_signal(barrier, inc=1, device_id=(r, (c + dc) % 16), device_id_type=MESH)
-    lax.fori_loop(1, 8, greet, 0)
+    def greet(row_, col_):
+        pl.semaphore_signal(barrier, inc=1, device_id=(row_, col_), device_id_type=MESH)
+
+    for d in range(1, 16):
+        greet(r, (c + d) % 16)
+    for d in range(1, 8):
+        greet((r + d) % 8, c)
+    for d in range(8):
+        greet(z * 2 + 1 - xl, (1 - xh) * 8 + d)
 
     dx = (k + xl) % 2
     p_xh = (xh + dx) % 2
@@ -99,11 +101,6 @@
         full_off.append(off)
         full_cp.append(cp)
 
-    def pick(n, carry):
-        sendbuf[n] = packed[slots[n]]
-        return carry
-    lax.fori_loop(0, 128, pick, 0, unroll=8)
-
     def turn_piece(read, off, store):
         i = lax.broadcasted_iota(jnp.int32, (256, 384), 0)
         lane = lax.broadcasted_iota(jnp.int32, (256, 384), 1)
@@ -132,9 +129,18 @@
 
     for n in range(2 * EARLY):
         stage_p1(n)
-    pl.semaphore_wait(barrier, 127)
+    pl.semaphore_wait(barrier, 30)
+    for d in range(1, 8):
+        pl.semaphore_signal(all_sem, inc=1, device_id=((r + d) % 8, c), device_id_type=MESH)
     for i in range(EARLY):
         send_p1(i)
+
+    def pick(n, carry):
+        sendbuf[n] = packed[slots[n]]
+        return carry
+    lax.fori_loop(0, 128, pick, 0, unroll=8)
+
+    pl.semaphore_wait(all_sem, 7)
 
     def give(to_r, to_c):
         to = to_r * 16 + to_c
@@ -460,7 +466,7 @@
             vm(6, KB, 384), vm(4, KB, 896), vm(6, SLOT, MAIN), vm(3, ROWS, MAIN), vm(16, ROWS, MAIN), vm(16, NROWS, NMAIN),
             vm(256, 2048), vm(2048, NPAD), vm(2048, NPAD), vm(NPAD, NPAD), vm(512, NPAD),
             pltpu.VMEM((ROWS, NPAD), F32), vm(4, 256, 256), vm(256, NPAD), pltpu.VMEM((512, 128), F32), pltpu.VMEM((512, 128), F32),
-            dma((6,)), dma((4,)), dma, dma, dma,
+            pltpu.SemaphoreType.REGULAR, dma((6,)), dma((4,)), dma, dma, dma,
             dma((6,)), dma((6,)), dma((3,)), dma((3,)),
             dma((6, 2, 2)), dma((6, 2, 2)), dma((6, 2)), dma((6, 2)), dma((6, 4)), dma((6, 4)), dma((1,)), dma((1,)),
             dma((19,)), dma((20,)),

time: 108 us -> 108 us (level)
  no operation moved by 1% of the time
where the time goes in v6:
time: 108 us
  Pallas kernels  99.8 us (92%)
  local copies, waits for them, and re-layouts  4.81 us (4%)
  other arithmetic  3.25 us (3%)
    pallas_call x1, Pallas kernels, body(): pl.pallas_call(kernel, out_shape=jax.ShapeDtypeStruct((TILE, TILE), BF),...  99.8 us
    unnamed x3, local copies, waits for them, and re-layouts  3.84 us

profile of v6, /device:TPU:1, one launch (start us, length us, event | category | flops | bytes accessed | tf_op | source)
XLA Modules:
  0.0 107.9 jit_solution(14482208454387686173)
XLA Ops:
  0.0 0.0 slice-start
  0.0 0.7 broadcast_compare_fusion
  0.7 1.5 %select_reduce_fusion.slots = s32[128]{0:T(128)} fusion(s32[128,128]{1,0:T(8,128)} %constant.17.clone, pred[128]{0:T(512)(128)(4,1)S(1)} %broadcast_compare_fusion), kind=kLoop, calls=%fused_computation.1 | loop fusion | flops 32640 | bytes 66176 | tf_op jit(solution)/shard_map/reduce_sum | solution.py:449
  2.2 1.0 slice.7
  3.2 0.3 copy.11
  3.5 0.0 slice-done
  3.5 1.0 copy.10
  4.5 1.1 pad_add_fusion.packed
  5.5 99.8 %shard_map.55 = bf16[800,800]{1,0:T(8,128)(2,1)} custom-call(s32[128]{0:T(128)} %select_reduce_fusion.slots, s32[128]{0:T(128)} %owner.1, bf16[400,12800]{1,0:T(8,128)(2,1)} %bitcast.2, bf16[72,32,128]{2,1,0:T(8,128)(2,1)} %pad_add_fusion.packed, s32[50,128]{1,0:T(8,128)} %bitcast.3), custom_call_target="tpu_custom_call" | custom-call | flops 8192000000 | bytes 20000000 | tf_op jit(solution)/shard_map/pallas_call | solution.py:458
  105.3 2.6 %copy.13 = bf16[800,800]{1,0:T(8,128)(2,1)} copy(bf16[800,800]{1,0:T(8,128)(2,1)} %shard_map.55) | data formatting | bytes 2560000
Async XLA Ops:
  0.0 3.5 %slice-start = ((bf16[72,50,50]{0,2,1:T(8,128)(2,1)}), bf16[72,32,50]{0,2,1:T(8,128)(2,1)S(1)}, s32[]{:S(2)}) async-start(bf16[72,50,50]{0,2,1:T(8,128)(2,1)} %param.6), calls=%async_computation | async-start | bytes 917504 | tf_op jit(solution)/shard_map/slice | solution.py:454
